TPU v7x, 32 devices: a whole 2x2x4 slice. The times are simulated.
32 devices in a mesh: fsdp: 8 (over z, y), ctx: 4 (over x, core).
Axes of the slice: x: 2, y: 2, z: 4, core: 2. Of those that a mesh axis runs over, the one named last changes fastest.
Arguments:
- tokens: bfloat16 [8, 2, 4, 384, 512], P('fsdp', None, 'ctx'), may hold values from -6 to 6
- query_weight: bfloat16 [512, 512], P('fsdp'), may hold values from -0.25 to 0.25
- query_bias: bfloat16 [512], P('fsdp'), may hold values from -1.796875 to 1.796875
- key_weight: bfloat16 [512, 512], P('fsdp'), may hold values from -0.25 to 0.25
- value_weight: bfloat16 [512, 512], P('fsdp'), may hold values from -0.25 to 0.25
- value_bias: bfloat16 [512], P('fsdp'), may hold values from -1.796875 to 1.796875
- out_weight: bfloat16 [512, 512], P('fsdp'), may hold values from -1 to 1
- out_bias: bfloat16 [512], P('fsdp'), may hold values from -1.796875 to 1.796875
- first_gain: bfloat16 [512], P('fsdp'), may hold values from 0.5 to 1.5
- first_shift: bfloat16 [512], P('fsdp'), may hold values from -1.796875 to 1.796875
- inner_weight: bfloat16 [512, 2048], P('fsdp'), may hold values from -0.25 to 0.25
- inner_bias: bfloat16 [2048], P('fsdp'), may hold values from -1.796875 to 1.796875
- outer_weight: bfloat16 [2048, 512], P('fsdp'), may hold values from -0.1875 to 0.1875
- outer_bias: bfloat16 [512], P('fsdp'), may hold values from -1.796875 to 1.796875
- second_gain: bfloat16 [512], P('fsdp'), may hold values from 0.5 to 1.5
- second_shift: bfloat16 [512], P('fsdp'), may hold values from -1.796875 to 1.796875
- cotangent: bfloat16 [8, 2, 4, 384, 512], P('fsdp', None, 'ctx'), may hold values from -6 to 6
Outputs:
- output: bfloat16 [8, 2, 4, 384, 512], P('fsdp', None, 'ctx')
- tokens_grad: bfloat16 [8, 2, 4, 384, 512], P('fsdp', None, 'ctx')
- query_weight_grad: float32 [512, 512], P('fsdp')
- query_bias_grad: float32 [512], P('fsdp')
- key_weight_grad: float32 [512, 512], P('fsdp')
- value_weight_grad: float32 [512, 512], P('fsdp')
- value_bias_grad: float32 [512], P('fsdp')
- out_weight_grad: float32 [512, 512], P('fsdp')
- out_bias_grad: float32 [512], P('fsdp')
- first_gain_grad: float32 [512], P('fsdp')
- first_shift_grad: float32 [512], P('fsdp')
- inner_weight_grad: float32 [512, 2048], P('fsdp')
- inner_bias_grad: float32 [2048], P('fsdp')
- outer_weight_grad: float32 [2048, 512], P('fsdp')
- outer_bias_grad: float32 [512], P('fsdp')
- second_gain_grad: float32 [512], P('fsdp')
- second_shift_grad: float32 [512], P('fsdp')
All inputs are finite; a program needn't handle non-finite values.
Results may differ from a plain program's by a relative error of at most 0.028.
Values may be sent and summed in bfloat16 or wider, within the bound.
A program may use at most 128 MiB of HBM per device.

v0:
```python
import math

import jax
import jax.numpy as jnp
from jax import lax
from jax.sharding import PartitionSpec as P

HEADS = 8
HEAD = 64


def layer_norm(rows, gain, shift):
    center = rows - jnp.mean(rows, axis=-1, keepdims=True)
    spread = jnp.mean(center * center, axis=-1, keepdims=True)
    return center * lax.rsqrt(spread + 1e-05) * gain + shift


def smooth_gate(values):
    return jax.nn.gelu(values, approximate=True)


def matmul_low(left, right):
    return jnp.dot(left, right, preferred_element_type=jnp.float32)


def times_transpose(left, right):
    return lax.dot_general(
        left, right, (((1,), (1,)), ((), ())), preferred_element_type=jnp.float32
    )


def column_sums(left, right):
    return lax.dot_general(
        left, right, (((0,), (0,)), ((), ())), preferred_element_type=jnp.float32
    )


def placements(row_index, device, block, block_count):
    half_index = row_index % (2 * block) // block
    within = row_index % block
    owner_block = jnp.where(half_index == 0, device, block_count - 1 - device)
    return owner_block * block + within


def shards(
    tokens,
    query_weight,
    query_bias,
    key_weight,
    value_weight,
    value_bias,
    out_weight,
    out_bias,
    first_gain,
    first_shift,
    inner_weight,
    inner_bias,
    outer_weight,
    outer_bias,
    second_gain,
    second_shift,
    cotangent,
):
    initials = (
        query_weight,
        query_bias,
        key_weight,
        value_weight,
        value_bias,
        out_weight,
        out_bias,
        first_gain,
        first_shift,
        inner_weight,
        inner_bias,
        outer_weight,
        outer_bias,
        second_gain,
        second_shift,
    )
    gathered = (
        lax.all_gather(query_weight, "fsdp", axis=0, tiled=True),
        lax.all_gather(query_bias, "fsdp", axis=0, tiled=True),
        lax.all_gather(key_weight, "fsdp", axis=0, tiled=True),
        lax.all_gather(value_weight, "fsdp", axis=0, tiled=True),
        lax.all_gather(value_bias, "fsdp", axis=0, tiled=True),
        lax.all_gather(out_weight, "fsdp", axis=0, tiled=True),
        lax.all_gather(out_bias, "fsdp", axis=0, tiled=True),
        lax.all_gather(first_gain, "fsdp", axis=0, tiled=True),
        lax.all_gather(first_shift, "fsdp", axis=0, tiled=True),
        lax.all_gather(inner_weight, "fsdp", axis=0, tiled=True),
        lax.all_gather(inner_bias, "fsdp", axis=0, tiled=True),
        lax.all_gather(outer_weight, "fsdp", axis=0, tiled=True),
        lax.all_gather(outer_bias, "fsdp", axis=0, tiled=True),
        lax.all_gather(second_gain, "fsdp", axis=0, tiled=True),
        lax.all_gather(second_shift, "fsdp", axis=0, tiled=True),
    )
    (
        w_query,
        b_query,
        w_key,
        w_value,
        b_value,
        w_out,
        b_out,
        gain_one,
        shift_one,
        w_inner,
        b_inner,
        w_outer,
        b_outer,
        gain_two,
        shift_two,
    ) = gathered
    block = tokens.shape[3]
    width = tokens.shape[4]
    token_rows = tokens.reshape(-1, width)
    row_count = token_rows.shape[0]
    ctx_count = lax.axis_size("ctx")
    ctx_index = lax.axis_index("ctx")
    local_places = placements(jnp.arange(row_count), ctx_index, block, 2 * ctx_count)
    all_index = jnp.arange(ctx_count * row_count)
    key_places = placements(all_index, all_index // row_count, block, 2 * ctx_count)
    query = (matmul_low(token_rows, w_query) + b_query.astype(jnp.float32)).astype(jnp.bfloat16)
    keys = matmul_low(token_rows, w_key).astype(jnp.bfloat16)
    values = (matmul_low(token_rows, w_value) + b_value.astype(jnp.float32)).astype(jnp.bfloat16)
    all_keys, all_values = (
        lax.all_gather(keys, "ctx", axis=0, tiled=True),
        lax.all_gather(values, "ctx", axis=0, tiled=True),
    )
    head_count = HEADS
    head_size = HEAD
    scale = 1.0 / math.sqrt(head_size)
    item_count = 2 * head_count

    def scores_of(member):
        section = member // head_count
        column = member % head_count * head_size
        query_block = lax.dynamic_slice(query, (section * block, column), (block, head_size))
        key_head = lax.dynamic_slice_in_dim(all_keys, column, head_size, 1)
        value_head = lax.dynamic_slice_in_dim(all_values, column, head_size, 1)
        query_places = lax.dynamic_slice_in_dim(local_places, section * block, block)
        raw_scores = times_transpose(query_block, key_head)
        allowed = query_places[:, None] >= key_places[None, :]
        masked = jnp.where(allowed, raw_scores * scale, -1e30)
        return (masked, query_block, key_head, value_head)

    def attend(member):
        masked, query_block, key_head, value_head = scores_of(member)
        row_top = jnp.max(masked, axis=1, keepdims=True)
        row_total = jnp.sum(jnp.exp(masked - row_top), axis=1, keepdims=True)
        log_total = row_top + jnp.log(row_total)
        probs = jnp.exp(masked - log_total).astype(jnp.bfloat16)
        return (matmul_low(probs, value_head), log_total[:, 0])

    head_outs, log_totals = lax.map(attend, jnp.arange(item_count))
    mixed = (
        head_outs.reshape(2, head_count, block, head_size)
        .transpose(0, 2, 1, 3)
        .reshape(row_count, width)
    )
    mixed_low = mixed.astype(jnp.bfloat16)
    branch = matmul_low(mixed_low, w_out) + b_out.astype(jnp.float32)
    first_sum = token_rows.astype(jnp.float32) + branch
    middle, pull_first = jax.vjp(
        layer_norm, first_sum, gain_one.astype(jnp.float32), shift_one.astype(jnp.float32)
    )
    middle_low = middle.astype(jnp.bfloat16)
    hidden = matmul_low(middle_low, w_inner) + b_inner.astype(jnp.float32)
    active, pull_gate = jax.vjp(smooth_gate, hidden)
    active_low = active.astype(jnp.bfloat16)
    second = matmul_low(active_low, w_outer) + b_outer.astype(jnp.float32)
    second_sum = middle + second
    result, pull_second = jax.vjp(
        layer_norm, second_sum, gain_two.astype(jnp.float32), shift_two.astype(jnp.float32)
    )
    d_result = cotangent.reshape(-1, width).astype(jnp.float32)
    d_second_sum, d_gain_two, d_shift_two = pull_second(d_result)
    d_second = d_second_sum.astype(jnp.bfloat16)
    d_b_outer = jnp.sum(d_second.astype(jnp.float32), axis=0)
    d_w_outer = column_sums(active_low, d_second)
    d_active = times_transpose(d_second, w_outer)
    d_hidden = pull_gate(d_active)[0].astype(jnp.bfloat16)
    d_b_inner = jnp.sum(d_hidden.astype(jnp.float32), axis=0)
    d_w_inner = column_sums(middle_low, d_hidden)
    d_middle = d_second_sum + times_transpose(d_hidden, w_inner)
    d_first_sum, d_gain_one, d_shift_one = pull_first(d_middle)
    d_branch = d_first_sum.astype(jnp.bfloat16)
    d_b_out = jnp.sum(d_branch.astype(jnp.float32), axis=0)
    d_w_out = column_sums(mixed_low, d_branch)
    d_mixed = times_transpose(d_branch, w_out).astype(jnp.bfloat16)
    d_items = (
        d_mixed.reshape(2, block, head_count, head_size)
        .transpose(0, 2, 1, 3)
        .reshape(item_count, block, head_size)
    )

    def attend_back(carry, operands):
        key_acc, value_acc = carry
        member, log_total, d_heads = operands
        masked, query_block, key_head, value_head = scores_of(member)
        probs = jnp.exp(masked - log_total[:, None])
        d_probs = times_transpose(d_heads, value_head)
        center = jnp.sum(probs * d_probs, axis=1, keepdims=True)
        d_scores = (probs * (d_probs - center) * scale).astype(jnp.bfloat16)
        d_query_part = matmul_low(d_scores, key_head)
        column = member % head_count * head_size
        key_part = lax.dynamic_slice_in_dim(key_acc, column, head_size, 1) + column_sums(
            d_scores, query_block
        )
        value_part = lax.dynamic_slice_in_dim(value_acc, column, head_size, 1) + column_sums(
            probs.astype(jnp.bfloat16), d_heads
        )
        key_acc = lax.dynamic_update_slice_in_dim(key_acc, key_part, column, 1)
        value_acc = lax.dynamic_update_slice_in_dim(value_acc, value_part, column, 1)
        return ((key_acc, value_acc), d_query_part)

    zero_acc = jnp.zeros((ctx_count * row_count, width), jnp.float32)
    (key_acc, value_acc), d_query_items = lax.scan(
        attend_back, (zero_acc, zero_acc), (jnp.arange(item_count), log_totals, d_items)
    )
    own_keys, own_values = (
        lax.psum_scatter(
            key_acc.astype(jnp.bfloat16), "ctx", scatter_dimension=0, tiled=True
        ).astype(jnp.float32),
        lax.psum_scatter(
            value_acc.astype(jnp.bfloat16), "ctx", scatter_dimension=0, tiled=True
        ).astype(jnp.float32),
    )
    d_query = (
        d_query_items.reshape(2, head_count, block, head_size)
        .transpose(0, 2, 1, 3)
        .reshape(row_count, width)
    )
    d_query_low = d_query.astype(jnp.bfloat16)
    d_keys_low = own_keys.astype(jnp.bfloat16)
    d_values_low = own_values.astype(jnp.bfloat16)
    d_w_query = column_sums(token_rows, d_query_low)
    d_b_query = jnp.sum(d_query_low.astype(jnp.float32), axis=0)
    d_w_key = column_sums(token_rows, d_keys_low)
    d_w_value = column_sums(token_rows, d_values_low)
    d_b_value = jnp.sum(d_values_low.astype(jnp.float32), axis=0)
    d_tokens = (
        d_first_sum
        + times_transpose(d_query_low, w_query)
        + times_transpose(d_keys_low, w_key)
        + times_transpose(d_values_low, w_value)
    )
    fsdp_count = lax.axis_size("fsdp")
    gradients = (
        d_w_query,
        d_b_query,
        d_w_key,
        d_w_value,
        d_b_value,
        d_w_out,
        d_b_out,
        d_gain_one,
        d_shift_one,
        d_w_inner,
        d_b_inner,
        d_w_outer,
        d_b_outer,
        d_gain_two,
        d_shift_two,
    )
    packed = jnp.concatenate(
        [gradient.reshape(fsdp_count, -1) for gradient in gradients], axis=1
    ).reshape(-1)
    shares = lax.psum_scatter(packed, "fsdp", scatter_dimension=0, tiled=True)
    summed = lax.psum(shares.astype(jnp.bfloat16), "ctx").astype(jnp.float32)
    unpacked = []
    offset = 0
    for initial in initials:
        unpacked.append(summed[offset : offset + initial.size].reshape(initial.shape))
        offset = offset + initial.size
    output = result.astype(jnp.bfloat16).reshape(tokens.shape)
    tokens_grad = d_tokens.astype(jnp.bfloat16).reshape(tokens.shape)
    return (output, tokens_grad) + tuple(unpacked)


def solution(mesh):
    return jax.shard_map(
        shards,
        mesh=mesh,
        in_specs=(
            P("fsdp", None, "ctx", None, None),
            P("fsdp", None),
            P("fsdp"),
            P("fsdp", None),
            P("fsdp", None),
            P("fsdp"),
            P("fsdp", None),
            P("fsdp"),
            P("fsdp"),
            P("fsdp"),
            P("fsdp", None),
            P("fsdp"),
            P("fsdp", None),
            P("fsdp"),
            P("fsdp"),
            P("fsdp"),
            P("fsdp", None, "ctx", None, None),
        ),
        out_specs=(
            P("fsdp", None, "ctx", None, None),
            P("fsdp", None, "ctx", None, None),
            P("fsdp", None),
            P("fsdp"),
            P("fsdp", None),
            P("fsdp", None),
            P("fsdp"),
            P("fsdp", None),
            P("fsdp"),
            P("fsdp"),
            P("fsdp"),
            P("fsdp", None),
            P("fsdp"),
            P("fsdp", None),
            P("fsdp"),
            P("fsdp"),
            P("fsdp"),
        ),
        check_vma=False,
    )
```

profile of v0, /device:TPU:0, one launch (start us, length us, event | category | flops | bytes accessed | tf_op | source)
XLA Modules:
  0.0 1328.3 jit_solution(5054888284815932312)
XLA Ops:
  16.1 23.4 %all-reduce.9 = (bf16[512]{0:T(512)(128)(2,1)S(1)}, bf16[512]{0:T(512)(128)(2,1)S(1)}, bf16[512]{0:T(512)(128)(2,1)S(1)}, bf16[512]{0:T(512)(128)(2,1)S(1)}, bf1...) all-reduce(bf16[512]{0:T(512)(128)(2,1)S(1)} %dynamic-update-slice,, ...), channel_id=1, replica_groups=mesh['fsdp'=8,'ctx'=4] {'fsdp'}, use_global_device_ids=true, to_apply=%add | all-reduce | flops 4096 | bytes 16384
  39.5 31.7 %all_gather.55 = bf16[512,512]{1,0:T(8,128)(2,1)S(1)} all-gather(bf16[64,512]{1,0:T(8,128)(2,1)} %param.25), channel_id=1, replica_groups=mesh['fsdp'=8,'ctx'=4] {'fsdp'}, dimensions={0}, use_global_device_ids=true | all-gather | bytes 589824 | tf_op jit(solution)/shard_map/all_gather | solution.py:85
  74.7 31.2 %all_gather.53 = bf16[512,512]{1,0:T(8,128)(2,1)S(1)} all-gather(bf16[64,512]{1,0:T(8,128)(2,1)S(1)} %copy-done.26), channel_id=1, replica_groups=mesh['fsdp'=8,'ctx'=4] {'fsdp'}, dimensions={0}, use_global_device_ids=true | all-gather | bytes 589824 | tf_op jit(solution)/shard_map/all_gather | solution.py:84
  109.7 16.3 %all-gather = bf16[8,1,256]{2,1,0:T(2,128)(2,1)S(1)} all-gather(bf16[1,1,256]{2,1,0:T(2,128)(2,1)S(1)} %reshape.293), channel_id=1, replica_groups=mesh['fsdp'=8,'ctx'=4] {'fsdp'}, dimensions={0}, use_global_device_ids=true | all-gather | bytes 4608 | tf_op jit(solution)/shard_map/all_gather | solution.py:92
  126.0 31.9 %all_gather.51 = bf16[512,512]{1,0:T(8,128)(2,1)S(1)} all-gather(bf16[64,512]{1,0:T(8,128)(2,1)S(1)} %copy-done.27), channel_id=1, replica_groups=mesh['fsdp'=8,'ctx'=4] {'fsdp'}, dimensions={0}, use_global_device_ids=true | all-gather | bytes 589824 | tf_op jit(solution)/shard_map/all_gather | solution.py:82
  157.9 32.5 %all_gather.58 = bf16[512,512]{1,0:T(8,128)(2,1)S(1)} all-gather(bf16[64,512]{1,0:T(8,128)(2,1)S(1)} %copy-done.28), channel_id=1, replica_groups=mesh['fsdp'=8,'ctx'=4] {'fsdp'}, dimensions={0}, use_global_device_ids=true | all-gather | bytes 589824 | tf_op jit(solution)/shard_map/all_gather | solution.py:87
  191.2 144.1 %while.32 = (s32[]{:T(128)}, bf16[16,384,64]{1,2,0:T(8,128)(2,1)S(1)}, f32[16,384]{1,0:T(8,128)S(1)}, s32[16]{0:T(128)S(1)}, s32[768]{0:T(1024)S(1)}, /*index=5*...) while((s32[]{:T(128)}, ...), condition=%wide.region_3.4_spmd.clone, body=%wide.region_0.3_spmd.clone.sunk | while | flops 311521952 | bytes 15974368 | solution.py:156
  338.4 6.3 fusion.99
  344.7 5.5 fusion.110
  354.8 5.9 convert_reduce_fusion
  377.2 265.6 %while.33 = (s32[]{:T(128)}, f32[3072,512]{0,1:T(8,128)}, f32[3072,512]{0,1:T(8,128)}, bf16[16,384,64]{1,2,0:T(8,128)(2,1)}, s32[16]{0:T(128)S(1)}, /*index=5*/s...) while((s32[]{:T(128)}, f32[3072,512]{0,1:T(8,128)}, ...), condition=%wide.region_14.15_spmd.clone, body=%wide.region_12.14_spmd.clone.sunk | while | flops 768438912 | bytes 41427464 | solution.py:219
  642.8 5.0 convert_element_type.180
  650.0 5.5 convert_element_type.181
  656.6 8.0 fusion.101
  664.7 5.0 reshape.257
  669.7 5.8 fusion.97
  675.5 5.1 reshape.255
  707.5 17.8 %reduce-scatter.5.cloned.1.call-done = bf16[768,512]{0,1:T(8,128)(2,1)} async-done(((bf16[3072,512]{0,1:T(8,128)(2,1)}), bf16[768,512]{0,1:T(8,128)(2,1)}) %reduce-scatter.5.cloned.1.call-update) | async-done | bytes 786448 | tf_op jit(solution)/shard_map/reduce_scatter | solution.py:226
  733.5 4.4 dynamic-update-slice.10
  748.7 12.8 dynamic-update-slice.17
  762.9 12.4 dynamic-update-slice.19
  779.4 9.9 reshape.261
  789.3 487.9 %all-reduce.14 = bf16[3151872]{0:T(1024)(128)(2,1)} all-reduce(f32[3151872]{0:T(1024)} %reshape.261), channel_id=4, replica_groups=mesh['fsdp'=8,'ctx'=4] {'fsdp'}, use_global_device_ids=true, to_apply=%region_26.27.clone | all-reduce | flops 3151872 | bytes 18911232
  1283.5 28.2 %all-reduce.13.cloned.1.call-done = bf16[393984]{0:T(1024)(128)(2,1)} async-done(((bf16[393984]{0:T(1024)(128)(2,1)}), bf16[393984]{0:T(1024)(128)(2,1)}) %all-reduce.13.cloned.1.call-update) | async-done | bytes 787984 | tf_op jit(solution)/shard_map/psum | solution.py:271
  (500 shorter events, 434.4 us)
Async XLA Ops:
  7.2 99.5 %copy-start.6 = (bf16[1,2,1,384,512]{4,3,2,1,0:T(8,128)(2,1)S(1)}, bf16[1,2,1,384,512]{4,3,2,1,0:T(8,128)(2,1)}, u32[]{:S(2)}) copy-start(bf16[1,2,1,384,512]{4,3,2,1,0:T(8,128)(2,1)} %param.21) | copy-start | bytes 2359300
  7.2 67.5 %copy-start.26 = (bf16[64,512]{1,0:T(8,128)(2,1)S(1)}, bf16[64,512]{1,0:T(8,128)(2,1)}, u32[]{:S(2)}) copy-start(bf16[64,512]{1,0:T(8,128)(2,1)} %param.24) | copy-start | bytes 196612
  7.2 183.8 %all-gather.8.cloned.1.call-start = ((), (), s32[]{:S(2)}) async-start(), calls=%async_computation.3 | async-start | bytes 3932160 | tf_op jit(solution)/shard_map/all_gather | solution.py:129
  74.6 34.9 %copy-start.31 = (bf16[256]{0:T(256)(128)(2,1)S(1)}, bf16[256]{0:T(256)(128)(2,1)}, u32[]{:S(2)}) copy-start(bf16[256]{0:T(256)(128)(2,1)} %param.32) | copy-start | bytes 1540
  74.6 51.4 %copy-start.27 = (bf16[64,512]{1,0:T(8,128)(2,1)S(1)}, bf16[64,512]{1,0:T(8,128)(2,1)}, u32[]{:S(2)}) copy-start(bf16[64,512]{1,0:T(8,128)(2,1)} %param.22) | copy-start | bytes 196612
  74.6 83.3 %copy-start.28 = (bf16[64,512]{1,0:T(8,128)(2,1)S(1)}, bf16[64,512]{1,0:T(8,128)(2,1)}, u32[]{:S(2)}) copy-start(bf16[64,512]{1,0:T(8,128)(2,1)} %param.27) | copy-start | bytes 196612
  74.7 116.4 %all-gather.6.cloned.1.call-start = ((), (), s32[]{:S(2)}) async-start(), calls=%async_computation.2 | async-start | bytes 3932160 | tf_op jit(solution)/shard_map/all_gather | solution.py:128
  108.2 230.3 %all-gather.10.cloned.1.call-start = ((), (), s32[]{:S(2)}) async-start(), calls=%async_computation.4 | async-start | bytes 2359296 | tf_op jit(solution)/shard_map/all_gather | solution.py:91
  108.9 235.8 %all-gather.12.cloned.1.call-start = ((), (), s32[]{:S(2)}) async-start(), calls=%async_computation.5 | async-start | bytes 2359296 | tf_op jit(solution)/shard_map/all_gather | solution.py:93
  109.5 590.0 %reduce-scatter.3.cloned.1.call-start = ((), (), s32[]{:S(2)}) async-start(), calls=%async_computation.6 | async-start | bytes 3932160 | tf_op jit(solution)/shard_map/reduce_scatter | solution.py:223
  157.9 32.5 %copy-start.22 = (bf16[512,512]{1,0:T(8,128)(2,1)}, bf16[512,512]{1,0:T(8,128)(2,1)S(1)}, u32[]{:S(2)}) copy-start(bf16[512,512]{1,0:T(8,128)(2,1)S(1)} %all_gather.51) | copy-start | bytes 1572868
  338.1 24.9 %copy-start.3 = (f32[768,512]{1,0:T(8,128)}, f32[768,512]{1,0:T(8,128)S(1)}, u32[]{:S(2)}) copy-start(f32[768,512]{1,0:T(8,128)S(1)} %get-tuple-element.506) | copy-start | bytes 4718596
  344.7 5.9 copy-start.8
  353.2 7.4 copy-start.24
  354.8 5.9 copy-start.29
  647.8 77.5 %reduce-scatter.5.cloned.1.call-start = ((), (), s32[]{:S(2)}) async-start(), calls=%async_computation.7 | async-start | bytes 3932160 | tf_op jit(solution)/shard_map/reduce_scatter | solution.py:226
  655.5 656.2 %all-reduce.13.cloned.1.call-start = ((), (), s32[]{:S(2)}) async-start(), calls=%async_computation.8 | async-start | bytes 1576960 | tf_op jit(solution)/shard_map/psum | solution.py:271
  664.7 5.1 copy-start.4
  675.5 5.3 copy-start.15
  675.5 5.3 copy-start.17
  729.4 4.0 copy-start.12
  789.3 490.6 %copy-start.18 = (bf16[768,512]{0,1:T(8,128)(2,1)S(1)}, bf16[768,512]{0,1:T(8,128)(2,1)}, u32[]{:S(2)}) copy-start(bf16[768,512]{0,1:T(8,128)(2,1)} %reduce-scatter.3.cloned.1.call-done) | copy-start | bytes 2359300
  1277.2 4.5 copy-start.2
  1277.2 4.5 copy-start.10
  (16 other events, 29.4 us)
Sparse Core Ops, SparseCore 0:
  74.8 25.8 all-gather.7
  108.3 25.8 all-gather.5
  136.3 52.9 all-gather.9
  191.3 48.4 all-gather.11
  648.0 36.7 reduce-scatter.2
  687.3 37.9 reduce-scatter.4
  1279.9 31.6 all-reduce.12
where the time goes:
time: 1340 us; the launch traced here: 1330 us
  blocking collectives  655 us (49%)
  matrix products  323 us (24%)
  local copies, waits for them, and re-layouts  150 us (11%)
  loops' own time  85.1 us (6%)
  other arithmetic  51.6 us (4%)
  waiting for transfers between devices  47.4 us (4%)
  between operations  16.2 us (1%)
    unnamed x2, blocking collectives  511 us
    dot_general x54, matrix products, times_transpose(): lax.dot_general(left, right, (((1,), (1,)), ((), ())), preferred_element_...  128 us
    dot_general x38, matrix products, column_sums(): lax.dot_general(left, right, (((0,), (0,)), ((), ())), preferred_element_...  109 us
    dot_general x38, matrix products, matmul_low(): return jnp.dot(left, right, preferred_element_type=jnp.float32)  85.6 us
    unnamed x101, local copies, waits for them, and re-layouts  67.5 us
    another operation x1, loops' own time, shards(): head_outs, log_totals = lax.map(attend, jnp.arange(item_count))  42.8 us
    another operation x1, loops' own time, shards(): lax.scan(attend_back, (zero_acc, zero_acc), (jnp.arange(item_count), log_...  42.3 us
    all_gather x1, blocking collectives, shards(): lax.all_gather(out_weight, 'fsdp', axis=0, tiled=True)  32.5 us
  transfers between devices with their start and end apart: 7, of which 2 were waited for; matrix products, arithmetic and copies ran while one was open for 13% of the time, Pallas kernels for 0%

commit v1 on v0

v1 whole, which is shorter than its diff:
```python
import functools
import math

import jax
import jax.numpy as jnp
from jax import lax
from jax.experimental import pallas as pl
from jax.experimental.pallas import tpu as pltpu
from jax.sharding import PartitionSpec as P

HEADS = 8
HEAD = 64
D = 512
FF = 2048
CTX = 4
SHARDS = 8
EPS = 1e-5
BF = jnp.bfloat16
F32 = jnp.float32
QUERY_SCALE = math.log2(math.e) / math.sqrt(HEAD)
SCALE = 1.0 / math.sqrt(HEAD)
LN2 = math.log(2.0)
G1_ROWS = 288
G2_ROWS = 112


def dot(left, right, left_dim=1, right_dim=0):
    return lax.dot_general(
        left, right, (((left_dim,), (right_dim,)), ((), ())), preferred_element_type=F32
    )


def rows_mean(value):
    return jnp.mean(value, axis=-1, keepdims=True)


def layer(ring, blk, *refs):
    it = iter(refs)
    take = lambda count: [next(it) for _ in range(count)]
    tok, cot = take(2)
    weights_in = take(6)
    small_in = take(1 if ring else 2)
    out_ref, tg_ref = take(2)
    if ring:
        grads_out = take(6)
        gsm_ref = next(it)
    else:
        p1_out, p2_out = take(2)
    X, K, V = take(3)
    Wq, Wk, Wv, Wo, Wi, Wu = weights = take(6)
    vec, vec_inner = take(2)
    Q, QTa, dO, dOTa = take(4)
    VTa, KT = take(2)
    top, acc, OT = take(3)
    Hlow, n1, rstd1 = take(3)
    Z, dU, dF, dR, dA = take(5)
    dwk, dwv = take(2)
    dka, dva = n1.at[0], n1.at[1]
    sums, sums_inner = take(2)
    cot_v = next(it)
    tg_v = dO
    P1, P2 = take(2)
    sib_out, sib_in, rel_out, rel_in, far_out, far_in = take(6)
    load_sem, out_sem, xs, xr = take(4)
    ds, dr = take(2)
    if ring:
        small_all = next(it)
        RC1, RY1, RZ1, FX1, RX1, FIN1 = take(6)
        RC2, RY2, RZ2, FX2, RX2, FIN2 = take(6)
        zs, ys, cs, rr, rc, ms, mr, gs, gr = take(9)

    t = lax.axis_index("ctx")
    chip, core = t // 2, lax.rem(t, 2)
    sib = t + 1 - 2 * core
    far = lax.rem(t + 2, 4)
    c = t
    MESH = pl.DeviceIdType.MESH

    def to(ref, dst, send, recv, **where):
        return pltpu.make_async_remote_copy(
            src_ref=ref,
            dst_ref=dst,
            send_sem=send,
            recv_sem=recv,
            device_id=where,
            device_id_type=MESH,
        )

    def arrived(ref, sem):
        pltpu.make_async_copy(ref, ref, sem).wait()

    def left(ref, sem):
        pltpu.make_async_copy(ref, ref, sem).wait()

    peers = [{"ctx": sib}, {"ctx": far}]
    if ring:
        f = lax.axis_index("fsdp")
        z, y = f // 2, lax.rem(f, 2)
        fy = f + 1 - 2 * y
        zpeer = [lax.rem(z + dz, 4) * 2 + y for dz in (1, 2, 3)]
        peers += [{"fsdp": fy}] + [{"fsdp": zp} for zp in zpeer]

    own_blocks = [c, 7 - c]
    loads = []
    for sec in range(2):
        loads.append(
            pltpu.make_async_copy(tok.at[sec], X.at[own_blocks[sec]], load_sem.at[sec])
        )
        loads.append(
            pltpu.make_async_copy(cot.at[sec], cot_v.at[sec], load_sem.at[2 + sec])
        )
    for w in range(6):
        rows = weights_in[w].shape[0]
        dst = weights[w].at[pl.ds(f * rows, rows)] if ring else weights[w]
        loads.append(pltpu.make_async_copy(weights_in[w], dst, load_sem.at[4 + w]))
    if ring:
        loads.append(
            pltpu.make_async_copy(small_in[0], small_all.at[f], load_sem.at[10])
        )
    else:
        loads.append(pltpu.make_async_copy(small_in[0], vec, load_sem.at[10]))
        loads.append(pltpu.make_async_copy(small_in[1], vec_inner, load_sem.at[11]))
    for copy in loads:
        copy.start()

    barrier = pltpu.get_barrier_semaphore()
    for where in peers:
        pl.semaphore_signal(barrier, inc=1, device_id=where, device_id_type=MESH)
    pl.semaphore_wait(barrier, len(peers))

    for sec in range(2):
        b = own_blocks[sec]
        to(tok.at[sec], X.at[b], xs.at[sec], xr.at[b], ctx=sib).start()
    to(tok.at[0], X.at[c], xs.at[2], xr.at[c], ctx=far).start()

    @pl.when(chip == 1)
    def _():
        to(tok.at[1], X.at[7 - c], xs.at[3], xr.at[7 - c], ctx=far).start()

    if ring:
        def piece(w, s, half):
            rows = weights_in[w].shape[0]
            return weights[w].at[pl.ds(s * rows + half * (rows // 2), rows // 2)]

        def gather_start(w):
            rows = weights_in[w].shape[0]
            src = weights_in[w].at[pl.ds(core * (rows // 2), rows // 2)]
            for i in range(3):
                to(src, piece(w, f, core), zs.at[w, i], rr.at[w, f], fsdp=zpeer[i]).start()
            to(src, piece(w, f, core), ys.at[w, 0], rr.at[w, f], fsdp=fy).start()

        def gather_z(w):
            for i in range(3):
                s = zpeer[i]
                ref = piece(w, s, core)
                arrived(ref, rr.at[w, s])
                to(ref, ref, ys.at[w, 1 + i], rr.at[w, s], fsdp=fy).start()
                to(ref, ref, cs.at[w, i], rc.at[w, s], ctx=sib).start()

        def gather_y(w):
            for i in range(4):
                s = lax.rem(z + i, 4) * 2 + 1 - y
                ref = piece(w, s, core)
                arrived(ref, rr.at[w, s])
                to(ref, ref, cs.at[w, 3 + i], rc.at[w, s], ctx=sib).start()

        def gather_end(w):
            for i in range(1, 8):
                s = lax.rem(f + i, 8)
                arrived(piece(w, s, 1 - core), rc.at[w, s])
            loads[4 + w].wait()

        def gather_left(w):
            rows = weights_in[w].shape[0]
            ref = weights[w].at[pl.ds(0, rows // 2)]
            for i in range(3):
                left(ref, zs.at[w, i])
            for i in range(4):
                left(ref, ys.at[w, i])
            for i in range(7):
                left(ref, cs.at[w, i])

        for i in range(3):
            to(small_in[0], small_all.at[f], ms.at[i], mr.at[f], fsdp=zpeer[i]).start()
        to(small_in[0], small_all.at[f], ms.at[3], mr.at[f], fsdp=fy).start()
        for w in range(6):
            gather_start(w)
        for i in range(3):
            s = zpeer[i]
            arrived(small_all.at[s], mr.at[s])
            to(small_all.at[s], small_all.at[s], ms.at[4 + i], mr.at[s], fsdp=fy).start()
        for w in range(3):
            gather_z(w)
    else:
        for w in range(6):
            loads[4 + w].wait()

    def far_tokens():
        b = far
        arrived(X.at[b], xr.at[b])
        to(X.at[b], X.at[b], xs.at[4], xr.at[b], ctx=sib).start()

        @pl.when(chip == 0)
        def _():
            b = 7 - far
            arrived(X.at[b], xr.at[b])
            to(X.at[b], X.at[b], xs.at[5], xr.at[b], ctx=sib).start()

    if ring:
        for w in range(3):
            gather_y(w)
        for i in range(4):
            s = lax.rem(z + i, 4) * 2 + 1 - y
            arrived(small_all.at[s], mr.at[s])
        loads[10].wait()
        vec[...] = jnp.concatenate(
            [small_all[s][0:8, 0:64] for s in range(SHARDS)], axis=1
        )
        vec_inner[...] = jnp.concatenate(
            [small_all[s][8 + k : 9 + k] for s in range(SHARDS) for k in range(2)],
            axis=1,
        )
        for w in range(3):
            gather_end(w)
    else:
        loads[10].wait()
        loads[11].wait()
    b_query, b_value, b_out, gain1, shift1, b_outer, gain2, shift2 = (
        vec[pl.ds(j, 1), :] for j in range(8)
    )
    for sec in range(2):
        loads[2 * sec].wait()

    VTa[:, 64:80, :] = jnp.ones((HEADS, 16, blk), BF)
    for h in range(HEADS):
        other = (1 - h % 2) * 64
        for sec in range(2):
            QTa[sec, h, other : other + 64, :] = jnp.zeros((64, blk), BF)
            dOTa[sec, h, other : other + 64, :] = jnp.zeros((64, blk), BF)

    def queries(sec, _):
        x = X[jnp.where(sec == 0, c, 7 - c)]
        q = (dot(x, Wq[...]) + b_query) * QUERY_SCALE
        Q[sec] = q.astype(BF)
        qt = q.T.astype(BF)
        for h in range(HEADS):
            own = (h % 2) * 64
            QTa[sec, h, own : own + 64, :] = qt[h * 64 : h * 64 + 64]
        return 0

    lax.fori_loop(0, 2, queries, 0)

    lane = lax.broadcasted_iota(jnp.int32, (blk, 128), 1)
    key_at = lax.broadcasted_iota(jnp.int32, (blk, blk), 0)
    query_at = lax.broadcasted_iota(jnp.int32, (blk, blk), 1)

    def step_of(i):
        sec = lax.rem(i, 2)
        owner_core = jnp.where(i < 2, 1 - core, core)
        owner = jnp.where(i < 4, 2 * (1 - chip) + owner_core, jnp.where(i < 6, sib, t))
        kb = jnp.where(sec == 0, owner, 7 - owner)
        sent = (i >= 4) | (chip == 0) | (sec == 0)
        return sec, owner, kb, sent, sent & (kb <= 7 - c)

    top[...] = jnp.full(top.shape, -1e30, F32)
    acc[...] = jnp.zeros(acc.shape, F32)

    def attend(sec, kb, diagonal):
        for h in range(HEADS):
            p, a = h // 2, h % 2
            k_pair = K[kb, :, p * 128 : p * 128 + 128]
            k_head = jnp.where((lane < 64) == (a == 0), k_pair, jnp.zeros_like(k_pair))
            s = dot(k_head, QTa[sec, h])
            if diagonal:
                s = jnp.where(key_at <= query_at, s, -1e30)
            old = top[sec, h, 0:1, :]
            new = jnp.maximum(old, jnp.max(s, axis=0, keepdims=True))
            probs = jnp.exp2(s - new).astype(BF)
            shrink = jnp.exp2(old - new)
            acc[sec, h] = acc[sec, h] * shrink + dot(VTa[h], probs)
            top[sec, h] = jnp.broadcast_to(new, (8, blk))

    def keys_values(kb):
        x = X[kb]
        K[kb] = dot(x, Wk[...]).astype(BF)
        v = dot(x, Wv[...]) + b_value
        V[kb] = v.astype(BF)
        vt = v.T.astype(BF)
        for h in range(HEADS):
            VTa[h, 0:64, :] = vt[h * 64 : h * 64 + 64]

    def forward(n, _):
        i = jnp.where(n < 2, 6 + n, jnp.where(n < 4, 2 + n, jnp.where(n < 6, n - 2, n - 6)))
        _, _, kb, sent, used = step_of(i)

        @pl.when(n == 4)
        def _():
            far_tokens()

        if ring:
            for when, w in ((1, 3), (2, 4), (3, 5)):
                pl.when(n == when)(functools.partial(gather_z, w))
            for when, w in ((4, 3), (5, 4), (6, 5)):
                pl.when(n == when)(functools.partial(gather_y, w))

        @pl.when(sent & ((n == 2) | (n == 3) | (n >= 6)))
        def _():
            arrived(X.at[kb], xr.at[kb])

        @pl.when(used)
        def _():
            keys_values(kb)

        def section(sec, _):
            qb = jnp.where(sec == 0, c, 7 - c)

            @pl.when(used & (kb < qb))
            def _():
                attend(sec, kb, False)

            @pl.when(used & (kb == qb))
            def _():
                attend(sec, kb, True)

            return 0

        lax.fori_loop(0, 2, section, 0)
        return 0

    lax.fori_loop(0, 8, forward, 0)

    def finish(sec, _):
        for h in range(HEADS):
            other = (1 - h % 2) * 64
            total = acc[sec, h, 64:65, :]
            OT[sec, h * 64 : h * 64 + 64, :] = (acc[sec, h, 0:64, :] / total).astype(BF)
            low = -(top[sec, h, 0:1, :] + jnp.log2(total))
            parts = []
            for _ in range(3):
                parts.append(low.astype(BF))
                low = low - parts[-1].astype(F32)
            QTa[sec, h, other : other + 16, :] = jnp.concatenate(
                parts + [jnp.zeros((13, blk), BF)], axis=0
            )
        return 0

    lax.fori_loop(0, 2, finish, 0)
    if ring:
        for w in range(3, 6):
            gather_end(w)
    for sec in range(2):
        loads[2 * sec + 1].wait()

    sums[...] = jnp.zeros(sums.shape, F32)
    sums_inner[...] = jnp.zeros(sums_inner.shape, F32)
    ones = jnp.ones((16, blk), BF)

    def column_sum(value):
        return jnp.sum(value, axis=0, keepdims=True)

    def dense(sec, _):
        x = X[jnp.where(sec == 0, c, 7 - c)].astype(F32)
        r1 = x + dot(OT[sec], Wo[...], 0, 0) + b_out
        center = r1 - rows_mean(r1)
        rs1 = lax.rsqrt(rows_mean(center * center) + EPS)
        n1[sec] = center * rs1
        rstd1[sec] = rs1
        hid = center * rs1 * gain1 + shift1
        low = hid.astype(BF)
        Hlow[sec] = low
        c0 = math.sqrt(2.0 / math.pi)
        for cb in range(4):
            cols = slice(cb * 512, cb * 512 + 512)
            u = dot(Hlow[sec], Wi[:, cols]) + vec_inner[:, cols]
            uu = u * u
            th = jnp.tanh(c0 * u * (1.0 + 0.044715 * uu))
            half = 0.5 * (1.0 + th)
            Z[sec, :, cols] = (u * half).astype(BF)
            slope = half + 0.5 * u * (1.0 - th * th) * (c0 * (1.0 + 3 * 0.044715 * uu))
            dU[sec, :, cols] = slope.astype(BF)
        r2 = hid + dot(Z[sec], Wu[...]) + b_outer
        center = r2 - rows_mean(r2)
        rs2 = lax.rsqrt(rows_mean(center * center) + EPS)
        n2 = center * rs2
        g = cot_v[sec].astype(F32)
        cot_v[sec] = (n2 * gain2 + shift2).astype(BF)
        sums[6:7, :] += column_sum(g * n2)
        sums[7:8, :] += column_sum(g)
        g = g * gain2
        d_r2 = (g - rows_mean(g) - n2 * rows_mean(g * n2)) * rs2
        dR[sec] = d_r2
        d_f = d_r2.astype(BF)
        dF[sec] = d_f
        sums[5:6, :] += dot(ones, d_f)[0:1]
        for cb in range(4):
            cols = slice(cb * 512, cb * 512 + 512)
            d_u = (dot(dF[sec], Wu[cols, :], 1, 1) * dU[sec, :, cols].astype(F32)).astype(BF)
            dU[sec, :, cols] = d_u
            sums_inner[0:1, cols] += dot(ones, d_u)[0:1]
        d_h = dR[sec] + dot(dU[sec], Wi[...], 1, 1)
        nn1 = n1[sec]
        sums[3:4, :] += column_sum(d_h * nn1)
        sums[4:5, :] += column_sum(d_h)
        g = d_h * gain1
        d_r1 = (g - rows_mean(g) - nn1 * rows_mean(g * nn1)) * rstd1[sec]
        dR[sec] = d_r1
        d_a = d_r1.astype(BF)
        dA[sec] = d_a
        sums[2:3, :] += dot(ones, d_a)[0:1]
        dO[sec] = dot(dA[sec], Wo[...], 1, 1).astype(BF)
        d_ot = dot(Wo[...], dA[sec], 1, 1)
        for h in range(HEADS):
            own, other = (h % 2) * 64, (1 - h % 2) * 64
            part = d_ot[h * 64 : h * 64 + 64].astype(BF)
            dOTa[sec, h, own : own + 64, :] = part
            o = OT[sec, h * 64 : h * 64 + 64, :].astype(F32)
            rest = -column_sum(part.astype(F32) * o)
            parts = []
            for _ in range(3):
                parts.append(rest.astype(BF))
                rest = rest - parts[-1].astype(F32)
            dOTa[sec, h, other : other + 16, :] = jnp.concatenate(
                parts + [jnp.zeros((13, blk), BF)], axis=0
            )
        return 0

    lax.fori_loop(0, 2, dense, 0)
    out_copy = pltpu.make_async_copy(cot_v, out_ref, out_sem.at[0])
    out_copy.start()

    def both(ref, cols=slice(None)):
        return jnp.concatenate([ref[0, :, cols], ref[1, :, cols]], axis=0)

    for rb in range(4):
        part = dot(both(Z, slice(rb * 512, rb * 512 + 512)), both(dF), 0, 0).astype(BF)
        for k in range(4):
            s, half = 2 * rb + k // 2, k % 2
            P1[half, s % 2, s // 2, 32:160, :] = part[k * 128 : k * 128 + 128]
    for cb in range(4):
        part = dot(both(Hlow), both(dU, slice(cb * 512, cb * 512 + 512)), 0, 0).astype(BF)
        for s in range(SHARDS):
            for half in range(2):
                at = s * 64 + half * 32
                P1[half, s % 2, s // 2, 160 + cb * 32 : 192 + cb * 32, :] = part[at : at + 32]

    def by_owner(dst, value, row):
        for s in range(SHARDS):
            for half in range(2):
                at = s * 64 + half * 32
                dst[half, s % 2, s // 2, row : row + 32, :] = value[at : at + 32]

    ot = jnp.concatenate([OT[0], OT[1]], axis=1)
    by_owner(P1, dot(ot, both(dA)).astype(BF), 0)

    if ring:
        groups = (
            (P1, RC1, RY1, RZ1, FX1, RX1, FIN1),
            (P2, RC2, RY2, RZ2, FX2, RX2, FIN2),
        )

        def add_into(dst, *terms):
            total = dst[...].astype(F32)
            for term in terms:
                total = total + term[...].astype(F32)
            dst[...] = total.astype(BF)

        def reduce_core(g):
            mine, from_core = groups[g][:2]
            for k, yy in ((0, 1 - y), (1, y)):
                to(mine.at[1 - core, yy], from_core.at[k], gs.at[g, k], gr.at[g, k], ctx=sib).start()

        def reduce_y(g):
            mine, from_core, from_y = groups[g][:3]
            arrived(from_core.at[0], gr.at[g, 0])

            def body(k, _):
                add_into(mine.at[core, 1 - y, k], from_core.at[0, k])
                return 0

            lax.fori_loop(0, 4, body, 0)
            to(mine.at[core, 1 - y], from_y, gs.at[g, 2], gr.at[g, 2], fsdp=fy).start()

        def reduce_z(g):
            mine, from_core, from_y, from_z = groups[g][:4]
            arrived(from_core.at[1], gr.at[g, 1])
            arrived(from_y, gr.at[g, 2])

            def body(k, _):
                add_into(mine.at[core, y, k], from_core.at[1, k], from_y.at[k])
                return 0

            lax.fori_loop(0, 4, body, 0)
            for i in range(3):
                zz = lax.rem(z + 1 + i, 4)
                to(mine.at[core, y, zz], from_z.at[i], gs.at[g, 3 + i], gr.at[g, 3 + i], fsdp=zpeer[i]).start()

        def reduce_x(g):
            mine, _, _, from_z, pair, from_x, _ = groups[g]
            for i in range(3):
                arrived(from_z.at[i], gr.at[g, 3 + i])
            pair[...] = (
                mine[core, y, z].astype(F32)
                + from_z[0].astype(F32)
                + from_z[1].astype(F32)
                + from_z[2].astype(F32)
            ).astype(BF)
            to(pair, from_x, gs.at[g, 6], gr.at[g, 6], ctx=far).start()

        def reduce_last(g):
            pair, from_x, final = groups[g][4:]
            arrived(from_x, gr.at[g, 6])
            final[core] = (pair[...].astype(F32) + from_x[...].astype(F32)).astype(BF)
            to(final.at[core], final.at[core], gs.at[g, 7], gr.at[g, 7], ctx=sib).start()

        def reduce_left(g):
            mine, from_core, from_y, from_z, pair, from_x, final = groups[g]
            for k in range(2):
                left(from_core.at[k], gs.at[g, k])
            left(from_y, gs.at[g, 2])
            for i in range(3):
                left(from_z.at[i], gs.at[g, 3 + i])
            left(pair, gs.at[g, 6])
            left(final.at[0], gs.at[g, 7])

        reduce_core(0)

    acc[...] = jnp.zeros(acc.shape, F32)
    dwk[...] = jnp.zeros(dwk.shape, F32)
    dwv[...] = jnp.zeros(dwv.shape, F32)

    def attend_back(sec, kb, diagonal):
        for p in range(4):
            cols = slice(p * 128, p * 128 + 128)
            k_pair, v_pair = K[kb, :, cols], V[kb, :, cols]
            q_pair, do_pair = Q[sec, :, cols], dO[sec, :, cols]
            zero = jnp.zeros_like(q_pair)
            all_p, all_ds, all_q, all_do = [], [], [], []
            for a in range(2):
                h = 2 * p + a
                own = (lane < 64) == (a == 0)
                first = (1 - a) * 64
                one = jnp.where((lane >= first) & (lane < first + 3), 1.0, 0.0).astype(BF)
                s = dot(jnp.where(own, k_pair, one), QTa[sec, h])
                if diagonal:
                    s = jnp.where(key_at <= query_at, s, -1e30)
                probs = jnp.exp2(s)
                dp = dot(jnp.where(own, v_pair, one), dOTa[sec, h])
                d_s = (probs * dp).astype(BF)
                all_p.append(probs.astype(BF))
                all_ds.append(d_s)
                all_q.append(jnp.where(own, q_pair, zero))
                all_do.append(jnp.where(own, do_pair, zero))
                acc[sec, h, 0:64, :] += dot(KT[h * 64 : h * 64 + 64, :], d_s)
            dva[:, cols] += dot(jnp.concatenate(all_p, axis=1), jnp.concatenate(all_do, axis=0))
            dka[:, cols] += dot(jnp.concatenate(all_ds, axis=1), jnp.concatenate(all_q, axis=0))

    def relay(sec):
        arrived(rel_in.at[sec], dr.at[2 + sec])
        far_out[sec] = (far_out[sec].astype(F32) + rel_in[sec].astype(F32)).astype(BF)
        to(far_out.at[sec], far_in.at[sec], ds.at[4 + sec], dr.at[4 + sec], ctx=far).start()

    def backward(i, _):
        owner_sec, owner, kb, sent, used = step_of(i)

        @pl.when(used)
        def _():
            KT[...] = K[kb].astype(F32).T.astype(BF)
            dka[...] = jnp.zeros(dka.shape, F32)
            dva[...] = jnp.zeros(dva.shape, F32)

        def section(sec, _):
            qb = jnp.where(sec == 0, c, 7 - c)

            @pl.when(used & (kb < qb))
            def _():
                attend_back(sec, kb, False)

            @pl.when(used & (kb == qb))
            def _():
                attend_back(sec, kb, True)

            return 0

        lax.fori_loop(0, 2, section, 0)

        @pl.when(used)
        def _():
            dk = (dka[...] * LN2).astype(BF)
            dv = dva[...].astype(BF)
            x = X[kb]
            dwk[...] += dot(x, dk, 0, 0)
            dwv[...] += dot(x, dv, 0, 0)
            sums[1:2, :] += dot(ones, dv)[0:1]
            dx = dot(dk, Wk[...], 1, 1) + dot(dv, Wv[...], 1, 1)

            @pl.when(i < 2)
            def _():
                rel_out[owner_sec] = dx.astype(BF)
                to(rel_out.at[owner_sec], rel_in.at[owner_sec], ds.at[2 + owner_sec], dr.at[2 + owner_sec], ctx=sib).start()

            @pl.when((i == 2) | (i == 3))
            def _():
                far_out[owner_sec] = dx.astype(BF)

            @pl.when((i == 4) | (i == 5))
            def _():
                sib_out[owner_sec] = dx.astype(BF)
                to(sib_out.at[owner_sec], sib_in.at[owner_sec], ds.at[owner_sec], dr.at[owner_sec], ctx=sib).start()

            @pl.when(i >= 6)
            def _():
                dR[owner_sec] += dx

        @pl.when(i == 3)
        def _():
            relay(0)
            pl.when(chip == 0)(functools.partial(relay, 1))

        if ring:
            pl.when(i == 1)(functools.partial(reduce_y, 0))
            pl.when(i == 3)(functools.partial(reduce_z, 0))
            pl.when(i == 5)(functools.partial(reduce_x, 0))
            pl.when(i == 6)(functools.partial(reduce_last, 0))
        return 0

    lax.fori_loop(0, 8, backward, 0)

    def d_query(sec, _):
        dq = jnp.concatenate([acc[sec, h, 0:64, :] for h in range(HEADS)], axis=0)
        Q[sec] = (dq * SCALE).T.astype(BF)
        sums[0:1, :] += dot(ones, Q[sec])[0:1]
        return 0

    lax.fori_loop(0, 2, d_query, 0)
    xx = jnp.concatenate([X[c], X[7 - c]], axis=0)
    by_owner(P2, dot(xx, both(Q), 0, 0).astype(BF), 0)
    by_owner(P2, dwk[...].astype(BF), 32)
    by_owner(P2, dwv[...].astype(BF), 64)
    for s in range(SHARDS):
        row = jnp.concatenate(
            [sums[:, s * 64 : s * 64 + 64], jnp.zeros((8, 448), F32)], axis=1
        )
        P2[0, s % 2, s // 2, 96:112, :] = jnp.concatenate(
            [row, jnp.zeros((8, 512), F32)], axis=0
        ).astype(BF)
        row = jnp.concatenate(
            [sums_inner[:, s * 256 : s * 256 + 256], jnp.zeros((8, 256), F32)], axis=1
        )
        P2[1, s % 2, s // 2, 96:112, :] = jnp.concatenate(
            [row, jnp.zeros((8, 512), F32)], axis=0
        ).astype(BF)
    if ring:
        reduce_core(1)
        reduce_y(1)

    for sec in range(2):
        dx = dR[sec] + dot(Q[sec], Wq[...], 1, 1)
        tg_v[sec] = dx.astype(BF)
        dR[sec] = dx

    def add_incoming(ref, sem, sec):
        arrived(ref.at[sec], sem)
        dR[sec] += ref[sec].astype(F32)

    add_incoming(sib_in, dr.at[0], 0)
    pl.when(core == 1)(lambda: add_incoming(sib_in, dr.at[1], 1))
    add_incoming(far_in, dr.at[4], 0)
    pl.when(chip == 1)(lambda: add_incoming(far_in, dr.at[5], 1))
    for sec in range(2):
        tg_v[sec] = dR[sec].astype(BF)
    tg_copy = pltpu.make_async_copy(tg_v, tg_ref, out_sem.at[1])
    tg_copy.start()

    if ring:
        reduce_z(1)
        arrived(FIN1.at[1 - core], gr.at[0, 7])
        gq, gk, gv, go, gi, gu = grads_out
        for half in range(2):
            go[half * 32 : half * 32 + 32, :] = FIN1[half, 0:32, :].astype(F32)
            gu[half * 128 : half * 128 + 128, :] = FIN1[half, 32:160, :].astype(F32)
            for cb in range(4):
                gi[half * 32 : half * 32 + 32, cb * 512 : cb * 512 + 512] = FIN1[
                    half, 160 + cb * 32 : 192 + cb * 32, :
                ].astype(F32)
        reduce_x(1)
        reduce_last(1)
        for w in range(6):
            gather_left(w)
        for i in range(7):
            left(small_all.at[0], ms.at[i])
        reduce_left(0)
        arrived(FIN2.at[1 - core], gr.at[1, 7])
        for half in range(2):
            for ref, row in ((gq, 0), (gk, 32), (gv, 64)):
                ref[half * 32 : half * 32 + 32, :] = FIN2[half, row : row + 32, :].astype(F32)
        gsm_ref[0:8, :] = FIN2[0, 96:112, 0:128].astype(F32)[0:8]
        gsm_ref[8:9, :] = FIN2[1, 96:112, 0:128].astype(F32)[0:1]
        gsm_ref[9:10, :] = FIN2[1, 96:112, 128:256].astype(F32)[0:1]
        reduce_left(1)
    else:
        copies = [
            pltpu.make_async_copy(P1, p1_out, load_sem.at[0]),
            pltpu.make_async_copy(P2, p2_out, load_sem.at[1]),
        ]
        for copy in copies:
            copy.start()
        for copy in copies:
            copy.wait()

    block = X.at[0]
    for k in range(3):
        left(block, xs.at[k])
    pl.when(chip == 1)(lambda: left(block, xs.at[3]))
    left(block, xs.at[4])
    pl.when(chip == 0)(lambda: left(block, xs.at[5]))
    left(block, ds.at[0])
    pl.when(core == 0)(lambda: left(block, ds.at[1]))
    left(block, ds.at[2])
    pl.when(chip == 0)(lambda: left(block, ds.at[3]))
    left(block, ds.at[4])
    pl.when(chip == 0)(lambda: left(block, ds.at[5]))
    out_copy.wait()
    tg_copy.wait()


def run(ring, tokens, cotangent, weights, smalls):
    blk = tokens.shape[1]
    vm = lambda *shape: pltpu.VMEM(shape, BF)
    vf = lambda *shape: pltpu.VMEM(shape, F32)
    dma = lambda *shape: pltpu.SemaphoreType.DMA(shape)
    any_spec = pl.BlockSpec(memory_space=pl.ANY)
    vmem_spec = pl.BlockSpec(memory_space=pltpu.VMEM)
    outs = [jax.ShapeDtypeStruct(tokens.shape, BF)] * 2
    out_specs = [any_spec] * 2
    if ring:
        outs += [jax.ShapeDtypeStruct(w.shape, F32) for w in weights]
        outs += [jax.ShapeDtypeStruct((16, 128), F32)]
        out_specs += [vmem_spec] * 7
    else:
        outs += [
            jax.ShapeDtypeStruct((2, 2, 4, rows, D), BF) for rows in (G1_ROWS, G2_ROWS)
        ]
        out_specs += [any_spec] * 2
    scratch = [vm(8, blk, D)] * 3
    scratch += [vm(D, D)] * 4 + [vm(D, FF), vm(FF, D)]
    scratch += [vf(8, D), vf(1, FF)]
    scratch += [vm(2, blk, D), vm(2, HEADS, 128, blk)] * 2
    scratch += [vm(HEADS, 80, blk), vm(D, blk)]
    scratch += [vf(2, HEADS, 8, blk), vf(2, HEADS, 80, blk), vm(2, D, blk)]
    scratch += [vm(2, blk, D), vf(2, blk, D), vf(2, blk, 1)]
    scratch += [vm(2, blk, FF)] * 2 + [vm(2, blk, D), vf(2, blk, D), vm(2, blk, D)]
    scratch += [vf(D, D)] * 2
    scratch += [vf(8, D), vf(8, FF)]
    scratch += [vm(2, blk, D)]
    scratch += [vm(2, 2, 4, G1_ROWS, D), vm(2, 2, 4, G2_ROWS, D)]
    scratch += [vm(2, blk, D)] * 6
    scratch += [dma(12), dma(2), dma(6), dma(8)]
    scratch += [dma(6), dma(6)]
    if ring:
        scratch += [vf(SHARDS, 16, 128)]
        for rows in (G1_ROWS, G2_ROWS):
            scratch += [vm(2, 4, rows, D), vm(4, rows, D), vm(3, rows, D)]
            scratch += [vm(rows, D), vm(rows, D), vm(2, rows, D)]
        scratch += [dma(6, 3), dma(6, 4), dma(6, 7), dma(6, 8), dma(6, 8)]
        scratch += [dma(7), dma(8), dma(2, 8), dma(2, 8)]
    inputs = [tokens, cotangent, *weights, *smalls]
    return pl.pallas_call(
        functools.partial(layer, ring, blk),
        out_shape=outs,
        in_specs=[any_spec] * len(inputs),
        out_specs=out_specs,
        scratch_shapes=scratch,
        compiler_params=pltpu.CompilerParams(
            collective_id=0, has_side_effects=True, vmem_limit_bytes=63 << 20
        ),
        name="layer",
    )(*inputs)


def shards(tokens, *rest):
    (wq, bq, wk, wv, bv, wo, bo, g1, s1, wi, bi, wu, bu, g2, s2, cotangent) = rest
    blk = tokens.shape[3]
    tok = tokens.reshape(2, blk, D)
    cot = cotangent.reshape(2, blk, D)
    weights = (wq, wk, wv, wo, wi, wu)
    vectors = (bq, bv, bo, g1, s1, bu, g2, s2)
    ring = lax.axis_size("fsdp") == SHARDS
    if ring:
        stacked = jnp.stack([v.astype(F32) for v in vectors])
        stacked = jnp.pad(stacked, ((0, 0), (0, 64)))
        inner = jnp.pad(bi.astype(F32).reshape(2, 128), ((0, 6), (0, 0)))
        small = jnp.concatenate([stacked, inner], axis=0)
        res = run(True, tok, cot, weights, (small,))
        output, tokens_grad, gq, gk, gv, go, gi, gu, gsm = res
        gvec = [gsm[j, 0:64] for j in range(8)]
        gbi = gsm[8:10].reshape(256)
    else:
        gather = lambda w: lax.all_gather(w, "fsdp", axis=0, tiled=True)
        full = [gather(w) for w in weights]
        vec = jnp.stack([gather(v).astype(F32) for v in vectors])
        inner = gather(bi).astype(F32).reshape(1, FF)
        output, tokens_grad, p1, p2 = run(False, tok, cot, full, (vec, inner))

        def whole(part, rows):
            return part.transpose(2, 1, 0, 3, 4).reshape(SHARDS * 2 * rows, D)

        parts = [
            whole(p2[:, :, :, 0:32], 32),
            whole(p2[:, :, :, 32:64], 32),
            whole(p2[:, :, :, 64:96], 32),
            whole(p1[:, :, :, 0:32], 32),
            p1[:, :, :, 160:288]
            .reshape(2, 2, 4, 4, 32, D)
            .transpose(2, 1, 0, 4, 3, 5)
            .reshape(D, FF),
            whole(p1[:, :, :, 32:160], 128),
        ]
        vecs = p2[0, :, :, 96:104, 0:64].transpose(2, 1, 0, 3).reshape(8, D)
        inner = p2[1, :, :, 96, 0:256].transpose(1, 0, 2).reshape(FF)
        parts += [vecs[j] for j in range(8)] + [inner]
        count = lax.axis_size("fsdp")
        packed = jnp.concatenate(
            [part.astype(F32).reshape(count, -1) for part in parts], axis=1
        ).reshape(-1)
        shares = lax.psum_scatter(packed, "fsdp", scatter_dimension=0, tiled=True)
        summed = lax.psum(shares.astype(BF), "ctx").astype(F32)
        pieces, at = [], 0
        for initial in weights + vectors + (bi,):
            pieces.append(summed[at : at + initial.size].reshape(initial.shape))
            at = at + initial.size
        gq, gk, gv, go, gi, gu = pieces[:6]
        gvec, gbi = pieces[6:14], pieces[14]
    order = (gq, gvec[0], gk, gv, gvec[1], go, gvec[2], gvec[3], gvec[4], gi, gbi, gu)
    order += (gvec[5], gvec[6], gvec[7])
    return (output.reshape(tokens.shape), tokens_grad.reshape(tokens.shape)) + order


def solution(mesh):
    row = P("fsdp", None)
    one = P("fsdp")
    act = P("fsdp", None, "ctx", None, None)
    params = (row, one, row, row, one, row, one, one, one, row, one, row, one, one, one)
    return jax.shard_map(
        shards,
        mesh=mesh,
        in_specs=(act,) + params + (act,),
        out_specs=(act, act) + params,
        check_vma=False,
    )
```

time: 1340 us -> 212 us (0.16)
  blocking collectives: 655 us -> 0 us
  matrix products: 323 us -> 0 us
  Pallas kernels: 0 us -> 195 us
  local copies, waits for them, and re-layouts: 150 us -> 12.2 us
  loops' own time: 85.1 us -> 0 us
  other arithmetic: 51.6 us -> 0.6 us
  waiting for transfers between devices: 47.4 us -> 0 us
  between operations: 16.2 us -> 0.75 us
    unnamed x2 -> x0, blocking collectives: 511 us -> none
    dot_general x130 -> x0, matrix products: 323 us -> none  [the longest x54 128 us: times_transpose(): lax.dot_general(left, right, (((1,), (1,)), ((), ())), preferred_element_...]
    pallas_call x0 -> x1, Pallas kernels: none -> 195 us  [run(): pl.pallas_call(functools.partial(layer, ring, blk), out_shape=outs, in_sp...]
    all_gather x5 -> x0, blocking collectives: 144 us -> none  [the longest x1 32.5 us: shards(): lax.all_gather(out_weight, 'fsdp', axis=0, tiled=True)]
    another operation x2 -> x0, loops' own time: 85.1 us -> none  [the longest x1 42.8 us: shards(): head_outs, log_totals = lax.map(attend, jnp.arange(item_count))]
    unnamed x101 -> x40, local copies, waits for them, and re-layouts: 67.5 us -> 9.43 us
    reshape x23 -> x1, local copies, waits for them, and re-layouts: 35.6 us -> 1.24 us  [shards(): gbi = gsm[8:10].reshape(256)]
    convert_element_type x27 -> x0, other arithmetic: 31.2 us -> none  [the longest x16 20.7 us: attend_back(): d_scores = (probs * (d_probs - center) * scale).astype(jnp.bfloat16)]
  transfers between devices with their start and end apart: 7 -> 0, of which waited for: 2 -> 0; matrix products, arithmetic and copies ran while one was open for 13% -> 0% of each run, Pallas kernels for 0% -> 0%
where the time goes in v1:
time: 212 us; the launch traced here: 208 us
  Pallas kernels  195 us (92%)
  local copies, waits for them, and re-layouts  12.2 us (6%)
    pallas_call x1, Pallas kernels, run(): pl.pallas_call(functools.partial(layer, ring, blk), out_shape=outs, in_sp...  195 us
    unnamed x40, local copies, waits for them, and re-layouts  9.43 us

profile of v1, /device:TPU:0, one launch (start us, length us, event | category | flops | bytes accessed | tf_op | source)
XLA Modules:
  0.0 208.3 jit_solution(5656067575218374120)
XLA Ops:
  0.7 0.6 copy-done.14
  1.3 0.0 copy-done.10
  1.3 0.0 copy-done.11
  1.3 0.0 copy-done.12
  1.4 0.0 copy-done.13
  1.4 0.0 copy-done.7
  1.4 0.0 copy-done.8
  1.4 0.0 copy-done.9
  1.5 0.7 copy-done.15
  2.1 0.6 fusion.3.refs_8_
  2.7 194.7 %layer.1 = (bf16[2,384,512]{2,1,0:T(8,128)(2,1)}, bf16[2,384,512]{2,1,0:T(8,128)(2,1)}, f32[64,512]{1,0:T(8,128)}, f32[64,512]{1,0:T(8,128)}, f32[64,512]{1,0:T(...) custom-call(bf16[2,384,512]{2,1,0:T(8,128)(2,1)} %bitcast.37, ...), custom_call_target="tpu_custom_call" | custom-call | tf_op jit(solution)/shard_map/layer/pallas_call | solution.py:767
  197.4 1.5 slice_bitcast_fusion.1
  198.9 1.2 slice_bitcast_fusion
  200.2 2.1 %copy.44 = bf16[1,2,1,384,512]{4,3,2,1,0:T(8,128)(2,1)} copy(bf16[1,2,1,384,512]{4,3,2,1,0:T(8,128)(2,1)} %bitcast.36) | data formatting | bytes 1572864
  202.3 0.9 copy.45
  203.2 0.1 copy-done.6
  203.3 0.7 copy.46
  204.0 0.7 copy.47
  204.6 0.7 copy.48
  205.3 0.3 copy-done.3
  205.6 0.7 copy.49
  206.3 0.8 copy.50
  207.0 0.4 copy-done.1
  207.5 0.8 copy.51
  (21 shorter events, 0.1 us)
Async XLA Ops:
  0.7 0.7 copy-start.14
  0.7 0.7 copy-start.10
  0.7 0.7 copy-start.11
  0.7 0.7 copy-start.12
  0.7 0.7 copy-start.13
  0.7 0.7 copy-start.7
  0.7 0.7 copy-start.8
  0.7 0.7 copy-start.9
  1.5 0.7 copy-start.15
  200.2 2.1 %copy-start = (bf16[2,384,512]{2,1,0:T(8,128)(2,1)S(1)}, bf16[2,384,512]{2,1,0:T(8,128)(2,1)}, u32[]{:S(2)}) copy-start(bf16[2,384,512]{2,1,0:T(8,128)(2,1)} %get-tuple-element.27) | copy-start | bytes 2359300
  202.3 1.0 copy-start.6
  202.3 1.7 copy-start.5
  202.3 2.3 %copy-start.4 = (f32[64,512]{1,0:T(8,128)S(1)}, f32[64,512]{1,0:T(8,128)}, u32[]{:S(2)}) copy-start(f32[64,512]{1,0:T(8,128)} %get-tuple-element.82) | copy-start | bytes 393220
  203.3 2.9 %copy-start.2 = (f32[64,2048]{1,0:T(8,128)S(1)}, f32[64,2048]{1,0:T(8,128)}, u32[]{:S(2)}) copy-start(f32[64,2048]{1,0:T(8,128)} %get-tuple-element.88) | copy-start | bytes 1572868
  204.6 1.0 copy-start.3
  206.2 1.2 copy-start.1

commit v2 on v1

--- a/solution.py
+++ b/solution.py
@@ -20,8 +20,7 @@
 QUERY_SCALE = math.log2(math.e) / math.sqrt(HEAD)
 SCALE = 1.0 / math.sqrt(HEAD)
 LN2 = math.log(2.0)
-G1_ROWS = 288
-G2_ROWS = 112
+GROUP_ROWS = (128, 160, 112)
 
 
 def dot(left, right, left_dim=1, right_dim=0):
@@ -42,10 +41,9 @@
     small_in = take(1 if ring else 2)
     out_ref, tg_ref = take(2)
     if ring:
-        grads_out = take(6)
-        gsm_ref = next(it)
+        finals_out = take(3)
     else:
-        p1_out, p2_out = take(2)
+        pu_out, pi_out, pq_out = take(3)
     X, K, V = take(3)
     Wq, Wk, Wv, Wo, Wi, Wu = weights = take(6)
     vec, vec_inner = take(2)
@@ -59,14 +57,13 @@
     sums, sums_inner = take(2)
     cot_v = next(it)
     tg_v = dO
-    P1, P2 = take(2)
+    PU, PI, PQ = take(3)
     sib_out, sib_in, rel_out, rel_in, far_out, far_in = take(6)
     load_sem, out_sem, xs, xr = take(4)
     ds, dr = take(2)
     if ring:
         small_all = next(it)
-        RC1, RY1, RZ1, FX1, RX1, FIN1 = take(6)
-        RC2, RY2, RZ2, FX2, RX2, FIN2 = take(6)
+        buffers = [take(6) for _ in range(3)]
         zs, ys, cs, rr, rc, ms, mr, gs, gr = take(9)
 
     t = lax.axis_index("ctx")
@@ -183,7 +180,7 @@
         for i in range(3):
             to(small_in[0], small_all.at[f], ms.at[i], mr.at[f], fsdp=zpeer[i]).start()
         to(small_in[0], small_all.at[f], ms.at[3], mr.at[f], fsdp=fy).start()
-        for w in range(6):
+        for w in range(3):
             gather_start(w)
         for i in range(3):
             s = zpeer[i]
@@ -191,6 +188,8 @@
             to(small_all.at[s], small_all.at[s], ms.at[4 + i], mr.at[s], fsdp=fy).start()
         for w in range(3):
             gather_z(w)
+        for w in range(3, 6):
+            gather_start(w)
     else:
         for w in range(6):
             loads[4 + w].wait()
@@ -266,19 +265,33 @@
     acc[...] = jnp.zeros(acc.shape, F32)
 
     def attend(sec, kb, diagonal):
-        for h in range(HEADS):
+        def scores(h):
             p, a = h // 2, h % 2
             k_pair = K[kb, :, p * 128 : p * 128 + 128]
             k_head = jnp.where((lane < 64) == (a == 0), k_pair, jnp.zeros_like(k_pair))
             s = dot(k_head, QTa[sec, h])
             if diagonal:
                 s = jnp.where(key_at <= query_at, s, -1e30)
+            return s
+
+        def weigh(h, s):
             old = top[sec, h, 0:1, :]
             new = jnp.maximum(old, jnp.max(s, axis=0, keepdims=True))
-            probs = jnp.exp2(s - new).astype(BF)
-            shrink = jnp.exp2(old - new)
+            top[sec, h] = jnp.broadcast_to(new, (8, blk))
+            return jnp.exp2(s - new).astype(BF), jnp.exp2(old - new)
+
+        def gather_values(h, probs, shrink):
             acc[sec, h] = acc[sec, h] * shrink + dot(VTa[h], probs)
-            top[sec, h] = jnp.broadcast_to(new, (8, blk))
+
+        s = scores(0)
+        held = None
+        for h in range(HEADS):
+            later = scores(h + 1) if h + 1 < HEADS else None
+            now = (h, *weigh(h, s))
+            if held is not None:
+                gather_values(*held)
+            held, s = now, later
+        gather_values(*held)
 
     def keys_values(kb):
         x = X[kb]
@@ -428,35 +441,12 @@
     out_copy = pltpu.make_async_copy(cot_v, out_ref, out_sem.at[0])
     out_copy.start()
 
-    def both(ref, cols=slice(None)):
-        return jnp.concatenate([ref[0, :, cols], ref[1, :, cols]], axis=0)
-
-    for rb in range(4):
-        part = dot(both(Z, slice(rb * 512, rb * 512 + 512)), both(dF), 0, 0).astype(BF)
-        for k in range(4):
-            s, half = 2 * rb + k // 2, k % 2
-            P1[half, s % 2, s // 2, 32:160, :] = part[k * 128 : k * 128 + 128]
-    for cb in range(4):
-        part = dot(both(Hlow), both(dU, slice(cb * 512, cb * 512 + 512)), 0, 0).astype(BF)
-        for s in range(SHARDS):
-            for half in range(2):
-                at = s * 64 + half * 32
-                P1[half, s % 2, s // 2, 160 + cb * 32 : 192 + cb * 32, :] = part[at : at + 32]
-
-    def by_owner(dst, value, row):
-        for s in range(SHARDS):
-            for half in range(2):
-                at = s * 64 + half * 32
-                dst[half, s % 2, s // 2, row : row + 32, :] = value[at : at + 32]
-
-    ot = jnp.concatenate([OT[0], OT[1]], axis=1)
-    by_owner(P1, dot(ot, both(dA)).astype(BF), 0)
-
-    if ring:
-        groups = (
-            (P1, RC1, RY1, RZ1, FX1, RX1, FIN1),
-            (P2, RC2, RY2, RZ2, FX2, RX2, FIN2),
-        )
+    if ring:
+        groups = [(mine, *more) for mine, more in zip((PU, PI, PQ), buffers)]
+
+        finals = [
+            pltpu.make_async_copy(groups[g][6], finals_out[g], load_sem.at[g]) for g in range(3)
+        ]
 
         def add_into(dst, *terms):
             total = dst[...].astype(F32)
@@ -473,86 +463,139 @@
             mine, from_core, from_y = groups[g][:3]
             arrived(from_core.at[0], gr.at[g, 0])
 
-            def body(k, _):
+            def body(n, _):
+                k = lax.rem(z + 1 + n, 4)
                 add_into(mine.at[core, 1 - y, k], from_core.at[0, k])
+                to(mine.at[core, 1 - y, k], from_y.at[k], gs.at[g, 2 + n], gr.at[g, 2 + n], fsdp=fy).start()
                 return 0
 
             lax.fori_loop(0, 4, body, 0)
-            to(mine.at[core, 1 - y], from_y, gs.at[g, 2], gr.at[g, 2], fsdp=fy).start()
 
         def reduce_z(g):
             mine, from_core, from_y, from_z = groups[g][:4]
             arrived(from_core.at[1], gr.at[g, 1])
-            arrived(from_y, gr.at[g, 2])
-
-            def body(k, _):
+
+            def body(n, _):
+                k = lax.rem(z + 1 + n, 4)
+                arrived(from_y.at[k], gr.at[g, 2 + n])
                 add_into(mine.at[core, y, k], from_core.at[1, k], from_y.at[k])
+
+                @pl.when(n < 3)
+                def _():
+                    to(mine.at[core, y, k], from_z.at[n], gs.at[g, 6 + n], gr.at[g, 6 + n], fsdp=k * 2 + y).start()
+
                 return 0
 
             lax.fori_loop(0, 4, body, 0)
-            for i in range(3):
-                zz = lax.rem(z + 1 + i, 4)
-                to(mine.at[core, y, zz], from_z.at[i], gs.at[g, 3 + i], gr.at[g, 3 + i], fsdp=zpeer[i]).start()
 
         def reduce_x(g):
             mine, _, _, from_z, pair, from_x, _ = groups[g]
             for i in range(3):
-                arrived(from_z.at[i], gr.at[g, 3 + i])
+                arrived(from_z.at[i], gr.at[g, 6 + i])
             pair[...] = (
                 mine[core, y, z].astype(F32)
                 + from_z[0].astype(F32)
                 + from_z[1].astype(F32)
                 + from_z[2].astype(F32)
             ).astype(BF)
-            to(pair, from_x, gs.at[g, 6], gr.at[g, 6], ctx=far).start()
+            to(pair, from_x, gs.at[g, 9], gr.at[g, 9], ctx=far).start()
 
         def reduce_last(g):
             pair, from_x, final = groups[g][4:]
-            arrived(from_x, gr.at[g, 6])
+            arrived(from_x, gr.at[g, 9])
             final[core] = (pair[...].astype(F32) + from_x[...].astype(F32)).astype(BF)
-            to(final.at[core], final.at[core], gs.at[g, 7], gr.at[g, 7], ctx=sib).start()
-
-        def reduce_left(g):
+            to(final.at[core], final.at[core], gs.at[g, 10], gr.at[g, 10], ctx=sib).start()
+
+        def reduce_end(g):
             mine, from_core, from_y, from_z, pair, from_x, final = groups[g]
+            arrived(final.at[1 - core], gr.at[g, 10])
             for k in range(2):
                 left(from_core.at[k], gs.at[g, k])
-            left(from_y, gs.at[g, 2])
+            for i in range(4):
+                left(from_y.at[0], gs.at[g, 2 + i])
             for i in range(3):
-                left(from_z.at[i], gs.at[g, 3 + i])
-            left(pair, gs.at[g, 6])
-            left(final.at[0], gs.at[g, 7])
-
+                left(from_z.at[i], gs.at[g, 6 + i])
+            left(pair, gs.at[g, 9])
+            left(final.at[0], gs.at[g, 10])
+
+    def both(ref, cols=slice(None)):
+        return jnp.concatenate([ref[0, :, cols], ref[1, :, cols]], axis=0)
+
+    for rb in range(4):
+        part = dot(both(Z, slice(rb * 512, rb * 512 + 512)), both(dF), 0, 0).astype(BF)
+        for k in range(4):
+            s, half = 2 * rb + k // 2, k % 2
+            PU[half, s % 2, s // 2] = part[k * 128 : k * 128 + 128]
+    if ring:
         reduce_core(0)
+    for cb in range(4):
+        part = dot(both(Hlow), both(dU, slice(cb * 512, cb * 512 + 512)), 0, 0).astype(BF)
+        for s in range(SHARDS):
+            for half in range(2):
+                at = s * 64 + half * 32
+                PI[half, s % 2, s // 2, cb * 32 : cb * 32 + 32, :] = part[at : at + 32]
+
+    def by_owner(dst, value, row):
+        for s in range(SHARDS):
+            for half in range(2):
+                at = s * 64 + half * 32
+                dst[half, s % 2, s // 2, row : row + 32, :] = value[at : at + 32]
+
+    ot = jnp.concatenate([OT[0], OT[1]], axis=1)
+    by_owner(PI, dot(ot, both(dA)).astype(BF), 128)
+
+    if ring:
+        reduce_core(1)
+        reduce_y(0)
 
     acc[...] = jnp.zeros(acc.shape, F32)
     dwk[...] = jnp.zeros(dwk.shape, F32)
     dwv[...] = jnp.zeros(dwv.shape, F32)
 
     def attend_back(sec, kb, diagonal):
-        for p in range(4):
+        def scores(h):
+            p, a = h // 2, h % 2
+            own = (lane < 64) == (a == 0)
+            first = (1 - a) * 64
+            one = jnp.where((lane >= first) & (lane < first + 3), 1.0, 0.0).astype(BF)
             cols = slice(p * 128, p * 128 + 128)
-            k_pair, v_pair = K[kb, :, cols], V[kb, :, cols]
+            s = dot(jnp.where(own, K[kb, :, cols], one), QTa[sec, h])
+            if diagonal:
+                s = jnp.where(key_at <= query_at, s, -1e30)
+            return s, dot(jnp.where(own, V[kb, :, cols], one), dOTa[sec, h])
+
+        def weigh(s, dp):
+            probs = jnp.exp2(s)
+            return probs.astype(BF), (probs * dp).astype(BF)
+
+        def to_queries(h, d_s):
+            acc[sec, h, 0:64, :] += dot(KT[h * 64 : h * 64 + 64, :], d_s)
+
+        def to_keys(p, first, second):
+            cols = slice(p * 128, p * 128 + 128)
             q_pair, do_pair = Q[sec, :, cols], dO[sec, :, cols]
             zero = jnp.zeros_like(q_pair)
-            all_p, all_ds, all_q, all_do = [], [], [], []
-            for a in range(2):
-                h = 2 * p + a
-                own = (lane < 64) == (a == 0)
-                first = (1 - a) * 64
-                one = jnp.where((lane >= first) & (lane < first + 3), 1.0, 0.0).astype(BF)
-                s = dot(jnp.where(own, k_pair, one), QTa[sec, h])
-                if diagonal:
-                    s = jnp.where(key_at <= query_at, s, -1e30)
-                probs = jnp.exp2(s)
-                dp = dot(jnp.where(own, v_pair, one), dOTa[sec, h])
-                d_s = (probs * dp).astype(BF)
-                all_p.append(probs.astype(BF))
-                all_ds.append(d_s)
-                all_q.append(jnp.where(own, q_pair, zero))
-                all_do.append(jnp.where(own, do_pair, zero))
-                acc[sec, h, 0:64, :] += dot(KT[h * 64 : h * 64 + 64, :], d_s)
-            dva[:, cols] += dot(jnp.concatenate(all_p, axis=1), jnp.concatenate(all_do, axis=0))
-            dka[:, cols] += dot(jnp.concatenate(all_ds, axis=1), jnp.concatenate(all_q, axis=0))
+            low = lane < 64
+
+            def stacked(pair):
+                return jnp.concatenate(
+                    [jnp.where(low, pair, zero), jnp.where(low, zero, pair)], axis=0
+                )
+
+            dva[:, cols] += dot(jnp.concatenate([first[0], second[0]], axis=1), stacked(do_pair))
+            dka[:, cols] += dot(jnp.concatenate([first[1], second[1]], axis=1), stacked(q_pair))
+
+        now = scores(0)
+        done = []
+        for n in range(HEADS + 1):
+            later = scores(n + 1) if n + 1 < HEADS else None
+            if n < HEADS:
+                done.append(weigh(*now))
+            if n > 0:
+                to_queries(n - 1, done[n - 1][1])
+                if n % 2 == 0:
+                    to_keys(n // 2 - 1, done[n - 2], done[n - 1])
+            now = later
 
     def relay(sec):
         arrived(rel_in.at[sec], dr.at[2 + sec])
@@ -617,10 +660,10 @@
             pl.when(chip == 0)(functools.partial(relay, 1))
 
         if ring:
-            pl.when(i == 1)(functools.partial(reduce_y, 0))
-            pl.when(i == 3)(functools.partial(reduce_z, 0))
-            pl.when(i == 5)(functools.partial(reduce_x, 0))
-            pl.when(i == 6)(functools.partial(reduce_last, 0))
+            pl.when(i == 0)(functools.partial(reduce_y, 1))
+            pl.when(i == 2)(functools.partial(reduce_z, 0))
+            pl.when(i == 5)(functools.partial(reduce_z, 1))
+            pl.when(i == 6)(functools.partial(reduce_x, 0))
         return 0
 
     lax.fori_loop(0, 8, backward, 0)
@@ -633,25 +676,27 @@
 
     lax.fori_loop(0, 2, d_query, 0)
     xx = jnp.concatenate([X[c], X[7 - c]], axis=0)
-    by_owner(P2, dot(xx, both(Q), 0, 0).astype(BF), 0)
-    by_owner(P2, dwk[...].astype(BF), 32)
-    by_owner(P2, dwv[...].astype(BF), 64)
+    by_owner(PQ, dot(xx, both(Q), 0, 0).astype(BF), 0)
+    by_owner(PQ, dwk[...].astype(BF), 32)
+    by_owner(PQ, dwv[...].astype(BF), 64)
     for s in range(SHARDS):
         row = jnp.concatenate(
             [sums[:, s * 64 : s * 64 + 64], jnp.zeros((8, 448), F32)], axis=1
         )
-        P2[0, s % 2, s // 2, 96:112, :] = jnp.concatenate(
+        PQ[0, s % 2, s // 2, 96:112, :] = jnp.concatenate(
             [row, jnp.zeros((8, 512), F32)], axis=0
         ).astype(BF)
         row = jnp.concatenate(
             [sums_inner[:, s * 256 : s * 256 + 256], jnp.zeros((8, 256), F32)], axis=1
         )
-        P2[1, s % 2, s // 2, 96:112, :] = jnp.concatenate(
+        PQ[1, s % 2, s // 2, 96:112, :] = jnp.concatenate(
             [row, jnp.zeros((8, 512), F32)], axis=0
         ).astype(BF)
     if ring:
-        reduce_core(1)
-        reduce_y(1)
+        reduce_core(2)
+        reduce_x(1)
+        reduce_last(0)
+        reduce_y(2)
 
     for sec in range(2):
         dx = dR[sec] + dot(Q[sec], Wq[...], 1, 1)
@@ -672,35 +717,25 @@
     tg_copy.start()
 
     if ring:
-        reduce_z(1)
-        arrived(FIN1.at[1 - core], gr.at[0, 7])
-        gq, gk, gv, go, gi, gu = grads_out
-        for half in range(2):
-            go[half * 32 : half * 32 + 32, :] = FIN1[half, 0:32, :].astype(F32)
-            gu[half * 128 : half * 128 + 128, :] = FIN1[half, 32:160, :].astype(F32)
-            for cb in range(4):
-                gi[half * 32 : half * 32 + 32, cb * 512 : cb * 512 + 512] = FIN1[
-                    half, 160 + cb * 32 : 192 + cb * 32, :
-                ].astype(F32)
-        reduce_x(1)
         reduce_last(1)
+        reduce_z(2)
         for w in range(6):
             gather_left(w)
         for i in range(7):
             left(small_all.at[0], ms.at[i])
-        reduce_left(0)
-        arrived(FIN2.at[1 - core], gr.at[1, 7])
-        for half in range(2):
-            for ref, row in ((gq, 0), (gk, 32), (gv, 64)):
-                ref[half * 32 : half * 32 + 32, :] = FIN2[half, row : row + 32, :].astype(F32)
-        gsm_ref[0:8, :] = FIN2[0, 96:112, 0:128].astype(F32)[0:8]
-        gsm_ref[8:9, :] = FIN2[1, 96:112, 0:128].astype(F32)[0:1]
-        gsm_ref[9:10, :] = FIN2[1, 96:112, 128:256].astype(F32)[0:1]
-        reduce_left(1)
+        for g in range(2):
+            reduce_end(g)
+            finals[g].start()
+        reduce_x(2)
+        reduce_last(2)
+        reduce_end(2)
+        finals[2].start()
+        for g in range(3):
+            finals[g].wait()
     else:
         copies = [
-            pltpu.make_async_copy(P1, p1_out, load_sem.at[0]),
-            pltpu.make_async_copy(P2, p2_out, load_sem.at[1]),
+            pltpu.make_async_copy(part, out, load_sem.at[k])
+            for k, (part, out) in enumerate(((PU, pu_out), (PI, pi_out), (PQ, pq_out)))
         ]
         for copy in copies:
             copy.start()
@@ -729,18 +764,16 @@
     vf = lambda *shape: pltpu.VMEM(shape, F32)
     dma = lambda *shape: pltpu.SemaphoreType.DMA(shape)
     any_spec = pl.BlockSpec(memory_space=pl.ANY)
-    vmem_spec = pl.BlockSpec(memory_space=pltpu.VMEM)
     outs = [jax.ShapeDtypeStruct(tokens.shape, BF)] * 2
     out_specs = [any_spec] * 2
     if ring:
-        outs += [jax.ShapeDtypeStruct(w.shape, F32) for w in weights]
-        outs += [jax.ShapeDtypeStruct((16, 128), F32)]
-        out_specs += [vmem_spec] * 7
+        outs += [jax.ShapeDtypeStruct((2, rows, D), BF) for rows in GROUP_ROWS]
+        out_specs += [any_spec] * 3
     else:
         outs += [
-            jax.ShapeDtypeStruct((2, 2, 4, rows, D), BF) for rows in (G1_ROWS, G2_ROWS)
+            jax.ShapeDtypeStruct((2, 2, 4, rows, D), BF) for rows in GROUP_ROWS
         ]
-        out_specs += [any_spec] * 2
+        out_specs += [any_spec] * 3
     scratch = [vm(8, blk, D)] * 3
     scratch += [vm(D, D)] * 4 + [vm(D, FF), vm(FF, D)]
     scratch += [vf(8, D), vf(1, FF)]
@@ -752,17 +785,17 @@
     scratch += [vf(D, D)] * 2
     scratch += [vf(8, D), vf(8, FF)]
     scratch += [vm(2, blk, D)]
-    scratch += [vm(2, 2, 4, G1_ROWS, D), vm(2, 2, 4, G2_ROWS, D)]
+    scratch += [vm(2, 2, 4, rows, D) for rows in GROUP_ROWS]
     scratch += [vm(2, blk, D)] * 6
     scratch += [dma(12), dma(2), dma(6), dma(8)]
     scratch += [dma(6), dma(6)]
     if ring:
         scratch += [vf(SHARDS, 16, 128)]
-        for rows in (G1_ROWS, G2_ROWS):
+        for rows in GROUP_ROWS:
             scratch += [vm(2, 4, rows, D), vm(4, rows, D), vm(3, rows, D)]
             scratch += [vm(rows, D), vm(rows, D), vm(2, rows, D)]
         scratch += [dma(6, 3), dma(6, 4), dma(6, 7), dma(6, 8), dma(6, 8)]
-        scratch += [dma(7), dma(8), dma(2, 8), dma(2, 8)]
+        scratch += [dma(7), dma(8), dma(3, 11), dma(3, 11)]
     inputs = [tokens, cotangent, *weights, *smalls]
     return pl.pallas_call(
         functools.partial(layer, ring, blk),
@@ -777,6 +810,50 @@
     )(*inputs)
 
 
+def finish_kernel(out_in, tg_in, fu, fi, fq, *refs):
+    out_ref, tg_ref, gq, gk, gv, go, gi, gu = refs[:8]
+    vectors, inner = refs[8:16], refs[16]
+    sems = refs[17]
+    copies = [
+        pltpu.make_async_copy(out_in, out_ref, sems.at[0]),
+        pltpu.make_async_copy(tg_in, tg_ref, sems.at[1]),
+    ]
+    for copy in copies:
+        copy.start()
+    for half in range(2):
+        rows = slice(half * 32, half * 32 + 32)
+        gu[half * 128 : half * 128 + 128, :] = fu[half].astype(F32)
+        for cb in range(4):
+            gi[rows, cb * 512 : cb * 512 + 512] = fi[half, cb * 32 : cb * 32 + 32, :].astype(F32)
+        go[rows, :] = fi[half, 128:160, :].astype(F32)
+        gq[rows, :] = fq[half, 0:32, :].astype(F32)
+        gk[rows, :] = fq[half, 32:64, :].astype(F32)
+        gv[rows, :] = fq[half, 64:96, :].astype(F32)
+    small = fq[0, 96:112, 0:128].astype(F32)
+    for j in range(8):
+        vectors[j][...] = small[j : j + 1, 0:64]
+    inner[...] = fq[1, 96:112, 0:256].astype(F32)[0:1]
+    for copy in copies:
+        copy.wait()
+
+
+def finish_all(tokens, weights, res):
+    any_spec = pl.BlockSpec(memory_space=pl.ANY)
+    vmem_spec = pl.BlockSpec(memory_space=pltpu.VMEM)
+    outs = [jax.ShapeDtypeStruct(tokens.shape, BF)] * 2
+    outs += [jax.ShapeDtypeStruct(w.shape, F32) for w in weights]
+    outs += [jax.ShapeDtypeStruct((1, 64), F32)] * 8
+    outs += [jax.ShapeDtypeStruct((1, 256), F32)]
+    return pl.pallas_call(
+        finish_kernel,
+        out_shape=outs,
+        in_specs=[vmem_spec] * 5,
+        out_specs=[any_spec] * 2 + [vmem_spec] * 15,
+        scratch_shapes=[pltpu.SemaphoreType.DMA((2,))],
+        name="finish",
+    )(*res)
+
+
 def shards(tokens, *rest):
     (wq, bq, wk, wv, bv, wo, bo, g1, s1, wi, bi, wu, bu, g2, s2, cotangent) = rest
     blk = tokens.shape[3]
@@ -791,32 +868,33 @@
         inner = jnp.pad(bi.astype(F32).reshape(2, 128), ((0, 6), (0, 0)))
         small = jnp.concatenate([stacked, inner], axis=0)
         res = run(True, tok, cot, weights, (small,))
-        output, tokens_grad, gq, gk, gv, go, gi, gu, gsm = res
-        gvec = [gsm[j, 0:64] for j in range(8)]
-        gbi = gsm[8:10].reshape(256)
+        res = finish_all(tok, weights, res)
+        output, tokens_grad, gq, gk, gv, go, gi, gu = res[:8]
+        gvec = [v.reshape(64) for v in res[8:16]]
+        gbi = res[16].reshape(256)
     else:
         gather = lambda w: lax.all_gather(w, "fsdp", axis=0, tiled=True)
         full = [gather(w) for w in weights]
         vec = jnp.stack([gather(v).astype(F32) for v in vectors])
         inner = gather(bi).astype(F32).reshape(1, FF)
-        output, tokens_grad, p1, p2 = run(False, tok, cot, full, (vec, inner))
+        output, tokens_grad, pu, pi, pq = run(False, tok, cot, full, (vec, inner))
 
         def whole(part, rows):
             return part.transpose(2, 1, 0, 3, 4).reshape(SHARDS * 2 * rows, D)
 
         parts = [
-            whole(p2[:, :, :, 0:32], 32),
-            whole(p2[:, :, :, 32:64], 32),
-            whole(p2[:, :, :, 64:96], 32),
-            whole(p1[:, :, :, 0:32], 32),
-            p1[:, :, :, 160:288]
+            whole(pq[:, :, :, 0:32], 32),
+            whole(pq[:, :, :, 32:64], 32),
+            whole(pq[:, :, :, 64:96], 32),
+            whole(pi[:, :, :, 128:160], 32),
+            pi[:, :, :, 0:128]
             .reshape(2, 2, 4, 4, 32, D)
             .transpose(2, 1, 0, 4, 3, 5)
             .reshape(D, FF),
-            whole(p1[:, :, :, 32:160], 128),
+            whole(pu, 128),
         ]
-        vecs = p2[0, :, :, 96:104, 0:64].transpose(2, 1, 0, 3).reshape(8, D)
-        inner = p2[1, :, :, 96, 0:256].transpose(1, 0, 2).reshape(FF)
+        vecs = pq[0, :, :, 96:104, 0:64].transpose(2, 1, 0, 3).reshape(8, D)
+        inner = pq[1, :, :, 96, 0:256].transpose(1, 0, 2).reshape(FF)
         parts += [vecs[j] for j in range(8)] + [inner]
         count = lax.axis_size("fsdp")
         packed = jnp.concatenate(

time: 212 us -> 151 us (0.71); the launches traced: 208 us -> 150 us
  Pallas kernels: 195 us -> 147 us
  local copies, waits for them, and re-layouts: 12.2 us -> 1.35 us
    pallas_call x1, Pallas kernels: 195 us -> 143 us  [run(): pl.pallas_call(functools.partial(layer, ring, blk), out_shape=outs, in_sp...]
    unnamed x40 -> x18, local copies, waits for them, and re-layouts: 9.43 us -> 1.32 us
    pallas_call x0 -> x1, Pallas kernels: none -> 3.93 us  [finish_all(): pl.pallas_call(finish_kernel, out_shape=outs, in_specs=[vmem_spec] * 5, o...]
where the time goes in v2:
time: 151 us; the launch traced here: 150 us
  Pallas kernels  147 us (97%)
    pallas_call x1, Pallas kernels, run(): pl.pallas_call(functools.partial(layer, ring, blk), out_shape=outs, in_sp...  143 us
    pallas_call x1, Pallas kernels, finish_all(): pl.pallas_call(finish_kernel, out_shape=outs, in_specs=[vmem_spec] * 5, o...  3.93 us

profile of v2, /device:TPU:0, one launch (start us, length us, event | category | flops | bytes accessed | tf_op | source)
XLA Modules:
  0.0 150.3 jit_solution(7955303214340424354)
XLA Ops:
  0.7 0.0 copy-start.7
  0.7 0.0 copy-start.3
  0.7 0.0 copy-start.4
  0.7 0.0 copy-start.5
  0.7 0.0 copy-start.6
  0.7 0.0 copy-start
  0.7 0.0 copy-start.1
  0.7 0.0 copy-start.2
  0.7 0.6 copy-done.7
  1.3 0.0 copy-done.3
  1.3 0.0 copy-done.4
  1.3 0.0 copy-done.5
  1.4 0.0 copy-done.6
  1.4 0.0 copy-done
  1.4 0.0 copy-done.1
  1.4 0.0 copy-done.2
  1.4 0.0 copy-start.8
  1.5 0.6 copy-done.8
  2.1 0.6 fusion.3.refs_8_
  2.7 143.5 %layer.1 = (bf16[2,384,512]{2,1,0:T(8,128)(2,1)}, bf16[2,384,512]{2,1,0:T(8,128)(2,1)}, bf16[2,128,512]{2,1,0:T(8,128)(2,1)}, bf16[2,160,512]{2,1,0:T(8,128)(2,1)}, bf16[2,112,512]{2,1,0:T(8,128)(2,1)}) custom-call(bf16[2,384,512]{2,1,0:T(8,128)(2,1)} %bitcast.26, bf16[2,384,512]{2,1,0:T(8,128)(2,1)} %bitcast.27, bf16[64,512]{1,0:T(8,128)(2,1)} %refs_2_.1, ...), custom_call_target="tpu_custom_call" | custom-call | tf_op jit(solution)/shard_map/layer/pallas_call | solution.py:800
  146.2 3.9 %finish.1 = (bf16[2,384,512]{2,1,0:T(8,128)(2,1)}, bf16[2,384,512]{2,1,0:T(8,128)(2,1)}, f32[64,512]{1,0:T(8,128)}, f32[64,512]{1,0:T(8,128)}, f32[64,512]{1,0:T...) custom-call(bf16[2,384,512]{2,1,0:T(8,128)(2,1)} %get-tuple-element., ...), custom_call_target="tpu_custom_call" | custom-call | tf_op jit(solution)/shard_map/finish/pallas_call | solution.py:847
  (1 shorter events, 0.0 us)
Async XLA Ops:
  0.7 0.7 copy-start.7
  0.7 0.7 copy-start.3
  0.7 0.7 copy-start.4
  0.7 0.7 copy-start.5
  0.7 0.7 copy-start.6
  0.7 0.7 copy-start
  0.7 0.7 copy-start.1
  0.7 0.7 copy-start.2
  1.4 0.7 copy-start.8

commit v3 on v2

--- a/solution.py
+++ b/solution.py
@@ -20,7 +20,22 @@
 QUERY_SCALE = math.log2(math.e) / math.sqrt(HEAD)
 SCALE = 1.0 / math.sqrt(HEAD)
 LN2 = math.log(2.0)
-GROUP_ROWS = (128, 160, 112)
+AT_QUERY, AT_KEY, AT_VALUE, AT_SMALL, AT_OUT, AT_INNER, AT_OUTER, PACKED = 0, 32, 64, 96, 112, 144, 272, 400
+UNITS = ((0, 32), (32, 64), (64, 112), (112, 208), (208, 304), (304, 400))
+GATHER_AT = (
+    (0, 3, 1),
+    (1, 4, 1),
+    (2, 5, 1),
+    (3, 3, 2),
+    (4, 4, 2),
+    (6, 5, 2),
+    (7, 3, 3),
+    (9, 4, 3),
+    (11, 5, 3),
+    (12, 3, 0),
+    (15, 4, 0),
+)
+GROUP_ROWS = (128, 160, 64, 48)
 
 
 def dot(left, right, left_dim=1, right_dim=0):
@@ -37,15 +52,15 @@
     it = iter(refs)
     take = lambda count: [next(it) for _ in range(count)]
     tok, cot = take(2)
-    weights_in = take(6)
-    small_in = take(1 if ring else 2)
+    weights_in = take(7 if ring else 1)
+    small_in = take(0 if ring else 2)
     out_ref, tg_ref = take(2)
     if ring:
-        finals_out = take(3)
+        finals_out = take(4)
     else:
-        pu_out, pi_out, pq_out = take(3)
+        pu_out, pi_out, pk_out, pq_out = take(4)
     X, K, V = take(3)
-    Wq, Wk, Wv, Wo, Wi, Wu = weights = take(6)
+    W = next(it)
     vec, vec_inner = take(2)
     Q, QTa, dO, dOTa = take(4)
     VTa, KT = take(2)
@@ -57,14 +72,14 @@
     sums, sums_inner = take(2)
     cot_v = next(it)
     tg_v = dO
-    PU, PI, PQ = take(3)
-    sib_out, sib_in, rel_out, rel_in, far_out, far_in = take(6)
+    PU, PI, PK, PQ = take(4)
+    sib_in, rel_in, far_in = take(3)
+    sib_out, rel_out, far_out = dA, dF, Hlow
     load_sem, out_sem, xs, xr = take(4)
     ds, dr = take(2)
     if ring:
-        small_all = next(it)
-        buffers = [take(6) for _ in range(3)]
-        zs, ys, cs, rr, rc, ms, mr, gs, gr = take(9)
+        buffers = [take(6) for _ in range(4)]
+        zs, ys, cs, rz, ry, rc, gs, gr = take(8)
 
     t = lax.axis_index("ctx")
     chip, core = t // 2, lax.rem(t, 2)
@@ -106,17 +121,25 @@
         loads.append(
             pltpu.make_async_copy(cot.at[sec], cot_v.at[sec], load_sem.at[2 + sec])
         )
-    for w in range(6):
-        rows = weights_in[w].shape[0]
-        dst = weights[w].at[pl.ds(f * rows, rows)] if ring else weights[w]
-        loads.append(pltpu.make_async_copy(weights_in[w], dst, load_sem.at[4 + w]))
-    if ring:
-        loads.append(
-            pltpu.make_async_copy(small_in[0], small_all.at[f], load_sem.at[10])
-        )
+    if ring:
+        for w, at in enumerate((AT_QUERY, AT_KEY, AT_VALUE, AT_SMALL, AT_OUT, AT_OUTER)):
+            src = weights_in[w].at[core]
+            loads.append(
+                pltpu.make_async_copy(
+                    src, W.at[z, y, core, pl.ds(at, src.shape[0])], load_sem.at[4 + w]
+                )
+            )
+        for cb in range(4):
+            src = weights_in[6].at[core, :, pl.ds(cb * D, D)]
+            loads.append(
+                pltpu.make_async_copy(
+                    src, W.at[z, y, core, pl.ds(AT_INNER + cb * 32, 32)], load_sem.at[10 + cb]
+                )
+            )
     else:
-        loads.append(pltpu.make_async_copy(small_in[0], vec, load_sem.at[10]))
-        loads.append(pltpu.make_async_copy(small_in[1], vec_inner, load_sem.at[11]))
+        loads.append(pltpu.make_async_copy(weights_in[0], W, load_sem.at[4]))
+        loads.append(pltpu.make_async_copy(small_in[0], vec, load_sem.at[5]))
+        loads.append(pltpu.make_async_copy(small_in[1], vec_inner, load_sem.at[6]))
     for copy in loads:
         copy.start()
 
@@ -135,64 +158,66 @@
         to(tok.at[1], X.at[7 - c], xs.at[3], xr.at[7 - c], ctx=far).start()
 
     if ring:
-        def piece(w, s, half):
-            rows = weights_in[w].shape[0]
-            return weights[w].at[pl.ds(s * rows + half * (rows // 2), rows // 2)]
-
-        def gather_start(w):
-            rows = weights_in[w].shape[0]
-            src = weights_in[w].at[pl.ds(core * (rows // 2), rows // 2)]
-            for i in range(3):
-                to(src, piece(w, f, core), zs.at[w, i], rr.at[w, f], fsdp=zpeer[i]).start()
-            to(src, piece(w, f, core), ys.at[w, 0], rr.at[w, f], fsdp=fy).start()
-
-        def gather_z(w):
-            for i in range(3):
-                s = zpeer[i]
-                ref = piece(w, s, core)
-                arrived(ref, rr.at[w, s])
-                to(ref, ref, ys.at[w, 1 + i], rr.at[w, s], fsdp=fy).start()
-                to(ref, ref, cs.at[w, i], rc.at[w, s], ctx=sib).start()
-
-        def gather_y(w):
-            for i in range(4):
-                s = lax.rem(z + i, 4) * 2 + 1 - y
-                ref = piece(w, s, core)
-                arrived(ref, rr.at[w, s])
-                to(ref, ref, cs.at[w, 3 + i], rc.at[w, s], ctx=sib).start()
-
-        def gather_end(w):
-            for i in range(1, 8):
-                s = lax.rem(f + i, 8)
-                arrived(piece(w, s, 1 - core), rc.at[w, s])
-            loads[4 + w].wait()
-
-        def gather_left(w):
-            rows = weights_in[w].shape[0]
-            ref = weights[w].at[pl.ds(0, rows // 2)]
-            for i in range(3):
-                left(ref, zs.at[w, i])
-            for i in range(4):
-                left(ref, ys.at[w, i])
-            for i in range(7):
-                left(ref, cs.at[w, i])
-
-        for i in range(3):
-            to(small_in[0], small_all.at[f], ms.at[i], mr.at[f], fsdp=zpeer[i]).start()
-        to(small_in[0], small_all.at[f], ms.at[3], mr.at[f], fsdp=fy).start()
-        for w in range(3):
-            gather_start(w)
-        for i in range(3):
-            s = zpeer[i]
-            arrived(small_all.at[s], mr.at[s])
-            to(small_all.at[s], small_all.at[s], ms.at[4 + i], mr.at[s], fsdp=fy).start()
-        for w in range(3):
-            gather_z(w)
-        for w in range(3, 6):
-            gather_start(w)
+        def piece(u, zz, yy, half):
+            first, last = UNITS[u]
+            return W.at[zz, yy, half, pl.ds(first, last - first)]
+
+        def pieces(u, yy, half):
+            first, last = UNITS[u]
+            return W.at[:, yy, half, pl.ds(first, last - first)]
+
+        def gather_start(u):
+            ref = piece(u, z, y, core)
+            to(ref, ref, ys.at[u, z], ry.at[u], fsdp=fy).start()
+            pl.when(z < 3)(lambda: to(ref, ref, zs.at[u, 4], rz.at[u, z], fsdp=f + 2).start())
+            pl.when(z > 0)(lambda: to(ref, ref, zs.at[u, 5], rz.at[u, z], fsdp=f - 2).start())
+
+        def gather_z(u, hops):
+            def pass_on(zz, more, onward):
+                ref = piece(u, zz, y, core)
+                arrived(ref, rz.at[u, zz])
+                if hops < 3:
+                    pl.when(more)(lambda: to(ref, ref, zs.at[u, zz], rz.at[u, zz], fsdp=onward).start())
+                to(ref, ref, ys.at[u, zz], ry.at[u], fsdp=fy).start()
+
+            pl.when(z - hops >= 0)(lambda: pass_on(z - hops, z < 3, f + 2))
+            pl.when(z + hops <= 3)(lambda: pass_on(z + hops, z > 0, f - 2))
+            if hops == 3:
+                ref = pieces(u, y, core)
+                to(ref, ref, cs.at[u, 0], rc.at[u, 0], ctx=sib).start()
+
+        def gather_y(u):
+            ref = pieces(u, 1 - y, core)
+            arrived(ref, ry.at[u])
+            to(ref, ref, cs.at[u, 1], rc.at[u, 1], ctx=sib).start()
+
+        def gather_end(u):
+            arrived(pieces(u, y, 1 - core), rc.at[u, 0])
+            arrived(pieces(u, 1 - y, 1 - core), rc.at[u, 1])
+
+        def gather_left(u):
+            ref = piece(u, 0, 0, 0)
+            pl.when(z < 3)(lambda: left(ref, zs.at[u, 4]))
+            pl.when(z > 0)(lambda: left(ref, zs.at[u, 5]))
+            for zz in range(4):
+                onward = ((zz < z) & (z < 3)) | ((zz > z) & (z > 0))
+                pl.when(onward)(lambda zz=zz: left(ref, zs.at[u, zz]))
+                left(ref, ys.at[u, zz])
+            for i in range(2):
+                left(pieces(u, 0, 0), cs.at[u, i])
+
+        for copy in loads[4:]:
+            copy.wait()
+        for u in range(3):
+            gather_start(u)
+        for hops in (1, 2, 3):
+            for u in range(3):
+                gather_z(u, hops)
+        for u in range(3, 6):
+            gather_start(u)
     else:
-        for w in range(6):
-            loads[4 + w].wait()
+        for copy in loads[4:]:
+            copy.wait()
 
     def far_tokens():
         b = far
@@ -206,24 +231,17 @@
             to(X.at[b], X.at[b], xs.at[5], xr.at[b], ctx=sib).start()
 
     if ring:
-        for w in range(3):
-            gather_y(w)
-        for i in range(4):
-            s = lax.rem(z + i, 4) * 2 + 1 - y
-            arrived(small_all.at[s], mr.at[s])
-        loads[10].wait()
-        vec[...] = jnp.concatenate(
-            [small_all[s][0:8, 0:64] for s in range(SHARDS)], axis=1
-        )
-        vec_inner[...] = jnp.concatenate(
-            [small_all[s][8 + k : 9 + k] for s in range(SHARDS) for k in range(2)],
-            axis=1,
-        )
-        for w in range(3):
-            gather_end(w)
-    else:
-        loads[10].wait()
-        loads[11].wait()
+        for u in range(3):
+            gather_y(u)
+        for u in range(3):
+            gather_end(u)
+        small = [[W[s // 2, s % 2, half, AT_SMALL:AT_OUT, :].astype(F32) for s in range(SHARDS)] for half in range(2)]
+        vec[...] = jnp.concatenate([part[0:8, 0:64] for part in small[0]], axis=1)
+        vec_inner[...] = jnp.concatenate([part[0:1, 0:256] for part in small[1]], axis=1)
+
+    def weight(at, rows=32):
+        return W[:, :, :, at : at + rows, :].reshape(SHARDS * 2 * rows, D)
+
     b_query, b_value, b_out, gain1, shift1, b_outer, gain2, shift2 = (
         vec[pl.ds(j, 1), :] for j in range(8)
     )
@@ -239,7 +257,7 @@
 
     def queries(sec, _):
         x = X[jnp.where(sec == 0, c, 7 - c)]
-        q = (dot(x, Wq[...]) + b_query) * QUERY_SCALE
+        q = (dot(x, weight(AT_QUERY)) + b_query) * QUERY_SCALE
         Q[sec] = q.astype(BF)
         qt = q.T.astype(BF)
         for h in range(HEADS):
@@ -295,8 +313,8 @@
 
     def keys_values(kb):
         x = X[kb]
-        K[kb] = dot(x, Wk[...]).astype(BF)
-        v = dot(x, Wv[...]) + b_value
+        K[kb] = dot(x, weight(AT_KEY)).astype(BF)
+        v = dot(x, weight(AT_VALUE)) + b_value
         V[kb] = v.astype(BF)
         vt = v.T.astype(BF)
         for h in range(HEADS):
@@ -310,12 +328,6 @@
         def _():
             far_tokens()
 
-        if ring:
-            for when, w in ((1, 3), (2, 4), (3, 5)):
-                pl.when(n == when)(functools.partial(gather_z, w))
-            for when, w in ((4, 3), (5, 4), (6, 5)):
-                pl.when(n == when)(functools.partial(gather_y, w))
-
         @pl.when(sent & ((n == 2) | (n == 3) | (n >= 6)))
         def _():
             arrived(X.at[kb], xr.at[kb])
@@ -326,6 +338,12 @@
 
         def section(sec, _):
             qb = jnp.where(sec == 0, c, 7 - c)
+            if ring:
+                for at, u, hops in GATHER_AT:
+                    if hops:
+                        pl.when(2 * n + sec == at)(functools.partial(gather_z, u, hops))
+                    else:
+                        pl.when(2 * n + sec == at)(functools.partial(gather_y, u))
 
             @pl.when(used & (kb < qb))
             def _():
@@ -357,10 +375,11 @@
             )
         return 0
 
+    if ring:
+        gather_y(5)
     lax.fori_loop(0, 2, finish, 0)
     if ring:
-        for w in range(3, 6):
-            gather_end(w)
+        gather_end(3)
     for sec in range(2):
         loads[2 * sec + 1].wait()
 
@@ -371,27 +390,39 @@
     def column_sum(value):
         return jnp.sum(value, axis=0, keepdims=True)
 
-    def dense(sec, _):
-        x = X[jnp.where(sec == 0, c, 7 - c)].astype(F32)
-        r1 = x + dot(OT[sec], Wo[...], 0, 0) + b_out
+    def dense(sec):
+        x = X[own_blocks[sec]].astype(F32)
+        r1 = x + dot(OT[sec], weight(AT_OUT), 0, 0) + b_out
+        yield
         center = r1 - rows_mean(r1)
         rs1 = lax.rsqrt(rows_mean(center * center) + EPS)
         n1[sec] = center * rs1
         rstd1[sec] = rs1
-        hid = center * rs1 * gain1 + shift1
-        low = hid.astype(BF)
-        Hlow[sec] = low
+        Hlow[sec] = (n1[sec] * gain1 + shift1).astype(BF)
+        yield
         c0 = math.sqrt(2.0 / math.pi)
+        columns = [slice(cb * 512, cb * 512 + 512) for cb in range(4)]
+
+        def hidden(cb):
+            if ring and sec == 0 and cb == 2:
+                gather_end(4)
+            return dot(Hlow[sec], weight(AT_INNER + 32 * cb)) + vec_inner[:, columns[cb]]
+
+        u = hidden(0)
         for cb in range(4):
-            cols = slice(cb * 512, cb * 512 + 512)
-            u = dot(Hlow[sec], Wi[:, cols]) + vec_inner[:, cols]
+            later = hidden(cb + 1) if cb < 3 else None
             uu = u * u
             th = jnp.tanh(c0 * u * (1.0 + 0.044715 * uu))
             half = 0.5 * (1.0 + th)
-            Z[sec, :, cols] = (u * half).astype(BF)
+            Z[sec, :, columns[cb]] = (u * half).astype(BF)
             slope = half + 0.5 * u * (1.0 - th * th) * (c0 * (1.0 + 3 * 0.044715 * uu))
-            dU[sec, :, cols] = slope.astype(BF)
-        r2 = hid + dot(Z[sec], Wu[...]) + b_outer
+            dU[sec, :, columns[cb]] = slope.astype(BF)
+            u = later
+        yield
+        if ring and sec == 0:
+            gather_end(5)
+        r2 = n1[sec] * gain1 + shift1 + dot(Z[sec], weight(AT_OUTER, 128)) + b_outer
+        yield
         center = r2 - rows_mean(r2)
         rs2 = lax.rsqrt(rows_mean(center * center) + EPS)
         n2 = center * rs2
@@ -405,12 +436,23 @@
         d_f = d_r2.astype(BF)
         dF[sec] = d_f
         sums[5:6, :] += dot(ones, d_f)[0:1]
+        yield
+
+        def d_active(cb):
+            rows = W[cb, :, :, AT_OUTER:PACKED, :].reshape(D, D)
+            return dot(dF[sec], rows, 1, 1)
+
+        now = d_active(0)
         for cb in range(4):
-            cols = slice(cb * 512, cb * 512 + 512)
-            d_u = (dot(dF[sec], Wu[cols, :], 1, 1) * dU[sec, :, cols].astype(F32)).astype(BF)
-            dU[sec, :, cols] = d_u
-            sums_inner[0:1, cols] += dot(ones, d_u)[0:1]
-        d_h = dR[sec] + dot(dU[sec], Wi[...], 1, 1)
+            later = d_active(cb + 1) if cb < 3 else None
+            d_u = (now * dU[sec, :, columns[cb]].astype(F32)).astype(BF)
+            dU[sec, :, columns[cb]] = d_u
+            sums_inner[0:1, columns[cb]] += dot(ones, d_u)[0:1]
+            now = later
+        yield
+        inner = jnp.concatenate([weight(AT_INNER + 32 * cb) for cb in range(4)], axis=1)
+        d_h = dR[sec] + dot(dU[sec], inner, 1, 1)
+        yield
         nn1 = n1[sec]
         sums[3:4, :] += column_sum(d_h * nn1)
         sums[4:5, :] += column_sum(d_h)
@@ -420,8 +462,10 @@
         d_a = d_r1.astype(BF)
         dA[sec] = d_a
         sums[2:3, :] += dot(ones, d_a)[0:1]
-        dO[sec] = dot(dA[sec], Wo[...], 1, 1).astype(BF)
-        d_ot = dot(Wo[...], dA[sec], 1, 1)
+        yield
+        dO[sec] = dot(dA[sec], weight(AT_OUT), 1, 1).astype(BF)
+        d_ot = dot(weight(AT_OUT), dA[sec], 1, 1)
+        yield
         for h in range(HEADS):
             own, other = (h % 2) * 64, (1 - h % 2) * 64
             part = d_ot[h * 64 : h * 64 + 64].astype(BF)
@@ -435,17 +479,20 @@
             dOTa[sec, h, other : other + 16, :] = jnp.concatenate(
                 parts + [jnp.zeros((13, blk), BF)], axis=0
             )
-        return 0
-
-    lax.fori_loop(0, 2, dense, 0)
+
+    running = [dense(0), dense(1)]
+    if not ring:
+        list(running.pop(0))
+    while running:
+        running = [work for work in running if next(work, 0) is None]
     out_copy = pltpu.make_async_copy(cot_v, out_ref, out_sem.at[0])
     out_copy.start()
 
     if ring:
-        groups = [(mine, *more) for mine, more in zip((PU, PI, PQ), buffers)]
+        groups = [(mine, *more) for mine, more in zip((PU, PI, PK, PQ), buffers)]
 
         finals = [
-            pltpu.make_async_copy(groups[g][6], finals_out[g], load_sem.at[g]) for g in range(3)
+            pltpu.make_async_copy(groups[g][6], finals_out[g], load_sem.at[g]) for g in range(4)
         ]
 
         def add_into(dst, *terms):
@@ -471,9 +518,10 @@
 
             lax.fori_loop(0, 4, body, 0)
 
-        def reduce_z(g):
+        def reduce_z(g, first=0, last=4):
             mine, from_core, from_y, from_z = groups[g][:4]
-            arrived(from_core.at[1], gr.at[g, 1])
+            if first == 0:
+                arrived(from_core.at[1], gr.at[g, 1])
 
             def body(n, _):
                 k = lax.rem(z + 1 + n, 4)
@@ -486,7 +534,7 @@
 
                 return 0
 
-            lax.fori_loop(0, 4, body, 0)
+            lax.fori_loop(first, last, body, 0)
 
         def reduce_x(g):
             mine, _, _, from_z, pair, from_x, _ = groups[g]
@@ -634,7 +682,7 @@
             dwk[...] += dot(x, dk, 0, 0)
             dwv[...] += dot(x, dv, 0, 0)
             sums[1:2, :] += dot(ones, dv)[0:1]
-            dx = dot(dk, Wk[...], 1, 1) + dot(dv, Wv[...], 1, 1)
+            dx = dot(dk, weight(AT_KEY), 1, 1) + dot(dv, weight(AT_VALUE), 1, 1)
 
             @pl.when(i < 2)
             def _():
@@ -661,12 +709,19 @@
 
         if ring:
             pl.when(i == 0)(functools.partial(reduce_y, 1))
-            pl.when(i == 2)(functools.partial(reduce_z, 0))
-            pl.when(i == 5)(functools.partial(reduce_z, 1))
+            pl.when(i == 2)(functools.partial(reduce_z, 0, 0, 2))
+            pl.when(i == 3)(functools.partial(reduce_z, 0, 2, 4))
+            pl.when(i == 5)(functools.partial(reduce_z, 1, 0, 2))
+            pl.when(i == 6)(functools.partial(reduce_z, 1, 2, 4))
             pl.when(i == 6)(functools.partial(reduce_x, 0))
         return 0
 
     lax.fori_loop(0, 8, backward, 0)
+
+    by_owner(PK, dwk[...].astype(BF), 0)
+    by_owner(PK, dwv[...].astype(BF), 32)
+    if ring:
+        reduce_core(2)
 
     def d_query(sec, _):
         dq = jnp.concatenate([acc[sec, h, 0:64, :] for h in range(HEADS)], axis=0)
@@ -677,29 +732,26 @@
     lax.fori_loop(0, 2, d_query, 0)
     xx = jnp.concatenate([X[c], X[7 - c]], axis=0)
     by_owner(PQ, dot(xx, both(Q), 0, 0).astype(BF), 0)
-    by_owner(PQ, dwk[...].astype(BF), 32)
-    by_owner(PQ, dwv[...].astype(BF), 64)
     for s in range(SHARDS):
         row = jnp.concatenate(
             [sums[:, s * 64 : s * 64 + 64], jnp.zeros((8, 448), F32)], axis=1
         )
-        PQ[0, s % 2, s // 2, 96:112, :] = jnp.concatenate(
+        PQ[0, s % 2, s // 2, 32:48, :] = jnp.concatenate(
             [row, jnp.zeros((8, 512), F32)], axis=0
         ).astype(BF)
         row = jnp.concatenate(
             [sums_inner[:, s * 256 : s * 256 + 256], jnp.zeros((8, 256), F32)], axis=1
         )
-        PQ[1, s % 2, s // 2, 96:112, :] = jnp.concatenate(
+        PQ[1, s % 2, s // 2, 32:48, :] = jnp.concatenate(
             [row, jnp.zeros((8, 512), F32)], axis=0
         ).astype(BF)
     if ring:
-        reduce_core(2)
-        reduce_x(1)
-        reduce_last(0)
+        reduce_core(3)
         reduce_y(2)
+        reduce_y(3)
 
     for sec in range(2):
-        dx = dR[sec] + dot(Q[sec], Wq[...], 1, 1)
+        dx = dR[sec] + dot(Q[sec], weight(AT_QUERY), 1, 1)
         tg_v[sec] = dx.astype(BF)
         dR[sec] = dx
 
@@ -717,25 +769,29 @@
     tg_copy.start()
 
     if ring:
+        reduce_z(2)
+        reduce_z(3)
+        reduce_x(1)
+        reduce_last(0)
+        for u in range(6):
+            gather_left(u)
         reduce_last(1)
-        reduce_z(2)
-        for w in range(6):
-            gather_left(w)
-        for i in range(7):
-            left(small_all.at[0], ms.at[i])
+        reduce_x(2)
+        reduce_x(3)
         for g in range(2):
             reduce_end(g)
             finals[g].start()
-        reduce_x(2)
         reduce_last(2)
-        reduce_end(2)
-        finals[2].start()
-        for g in range(3):
+        reduce_last(3)
+        for g in range(2, 4):
+            reduce_end(g)
+            finals[g].start()
+        for g in range(4):
             finals[g].wait()
     else:
         copies = [
             pltpu.make_async_copy(part, out, load_sem.at[k])
-            for k, (part, out) in enumerate(((PU, pu_out), (PI, pi_out), (PQ, pq_out)))
+            for k, (part, out) in enumerate(((PU, pu_out), (PI, pi_out), (PK, pk_out), (PQ, pq_out)))
         ]
         for copy in copies:
             copy.start()
@@ -768,14 +824,14 @@
     out_specs = [any_spec] * 2
     if ring:
         outs += [jax.ShapeDtypeStruct((2, rows, D), BF) for rows in GROUP_ROWS]
-        out_specs += [any_spec] * 3
+        out_specs += [any_spec] * 4
     else:
         outs += [
             jax.ShapeDtypeStruct((2, 2, 4, rows, D), BF) for rows in GROUP_ROWS
         ]
-        out_specs += [any_spec] * 3
+        out_specs += [any_spec] * 4
     scratch = [vm(8, blk, D)] * 3
-    scratch += [vm(D, D)] * 4 + [vm(D, FF), vm(FF, D)]
+    scratch += [vm(4, 2, 2, PACKED, D)]
     scratch += [vf(8, D), vf(1, FF)]
     scratch += [vm(2, blk, D), vm(2, HEADS, 128, blk)] * 2
     scratch += [vm(HEADS, 80, blk), vm(D, blk)]
@@ -786,16 +842,15 @@
     scratch += [vf(8, D), vf(8, FF)]
     scratch += [vm(2, blk, D)]
     scratch += [vm(2, 2, 4, rows, D) for rows in GROUP_ROWS]
-    scratch += [vm(2, blk, D)] * 6
-    scratch += [dma(12), dma(2), dma(6), dma(8)]
+    scratch += [vm(2, blk, D)] * 3
+    scratch += [dma(14), dma(2), dma(6), dma(8)]
     scratch += [dma(6), dma(6)]
     if ring:
-        scratch += [vf(SHARDS, 16, 128)]
         for rows in GROUP_ROWS:
             scratch += [vm(2, 4, rows, D), vm(4, rows, D), vm(3, rows, D)]
             scratch += [vm(rows, D), vm(rows, D), vm(2, rows, D)]
-        scratch += [dma(6, 3), dma(6, 4), dma(6, 7), dma(6, 8), dma(6, 8)]
-        scratch += [dma(7), dma(8), dma(3, 11), dma(3, 11)]
+        scratch += [dma(6, 6), dma(6, 4), dma(6, 2), dma(6, 4), dma(6), dma(6, 2)]
+        scratch += [dma(4, 11), dma(4, 11)]
     inputs = [tokens, cotangent, *weights, *smalls]
     return pl.pallas_call(
         functools.partial(layer, ring, blk),
@@ -810,7 +865,7 @@
     )(*inputs)
 
 
-def finish_kernel(out_in, tg_in, fu, fi, fq, *refs):
+def finish_kernel(out_in, tg_in, fu, fi, fk, fq, *refs):
     out_ref, tg_ref, gq, gk, gv, go, gi, gu = refs[:8]
     vectors, inner = refs[8:16], refs[16]
     sems = refs[17]
@@ -827,12 +882,12 @@
             gi[rows, cb * 512 : cb * 512 + 512] = fi[half, cb * 32 : cb * 32 + 32, :].astype(F32)
         go[rows, :] = fi[half, 128:160, :].astype(F32)
         gq[rows, :] = fq[half, 0:32, :].astype(F32)
-        gk[rows, :] = fq[half, 32:64, :].astype(F32)
-        gv[rows, :] = fq[half, 64:96, :].astype(F32)
-    small = fq[0, 96:112, 0:128].astype(F32)
+        gk[rows, :] = fk[half, 0:32, :].astype(F32)
+        gv[rows, :] = fk[half, 32:64, :].astype(F32)
+    small = fq[0, 32:48, 0:128].astype(F32)
     for j in range(8):
         vectors[j][...] = small[j : j + 1, 0:64]
-    inner[...] = fq[1, 96:112, 0:256].astype(F32)[0:1]
+    inner[...] = fq[1, 32:48, 0:256].astype(F32)[0:1]
     for copy in copies:
         copy.wait()
 
@@ -847,7 +902,7 @@
     return pl.pallas_call(
         finish_kernel,
         out_shape=outs,
-        in_specs=[vmem_spec] * 5,
+        in_specs=[vmem_spec] * 6,
         out_specs=[any_spec] * 2 + [vmem_spec] * 15,
         scratch_shapes=[pltpu.SemaphoreType.DMA((2,))],
         name="finish",
@@ -863,29 +918,35 @@
     vectors = (bq, bv, bo, g1, s1, bu, g2, s2)
     ring = lax.axis_size("fsdp") == SHARDS
     if ring:
-        stacked = jnp.stack([v.astype(F32) for v in vectors])
-        stacked = jnp.pad(stacked, ((0, 0), (0, 64)))
-        inner = jnp.pad(bi.astype(F32).reshape(2, 128), ((0, 6), (0, 0)))
-        small = jnp.concatenate([stacked, inner], axis=0)
-        res = run(True, tok, cot, weights, (small,))
+        stacked = jnp.pad(jnp.stack(vectors), ((0, 8), (0, D - 64)))
+        inner = jnp.pad(bi.reshape(1, 256), ((0, 15), (0, D - 256)))
+        small = jnp.stack([stacked, inner])
+        halves = [w.reshape(2, -1, D) for w in (wq, wk, wv)] + [small]
+        halves += [wo.reshape(2, -1, D), wu.reshape(2, -1, D), wi.reshape(2, -1, FF)]
+        res = run(True, tok, cot, halves, ())
         res = finish_all(tok, weights, res)
         output, tokens_grad, gq, gk, gv, go, gi, gu = res[:8]
         gvec = [v.reshape(64) for v in res[8:16]]
         gbi = res[16].reshape(256)
     else:
         gather = lambda w: lax.all_gather(w, "fsdp", axis=0, tiled=True)
-        full = [gather(w) for w in weights]
+        rows = lambda w: gather(w).reshape(4, 2, 2, -1, D)
+        inner_rows = gather(wi).reshape(4, 2, 2, 32, 4, D).transpose(0, 1, 2, 4, 3, 5)
+        unused = jnp.zeros((4, 2, 2, AT_OUT - AT_SMALL, D), BF)
+        packed = [rows(wq), rows(wk), rows(wv), unused, rows(wo)]
+        packed += [inner_rows.reshape(4, 2, 2, 128, D), rows(wu)]
+        full = [jnp.concatenate(packed, axis=3)]
         vec = jnp.stack([gather(v).astype(F32) for v in vectors])
         inner = gather(bi).astype(F32).reshape(1, FF)
-        output, tokens_grad, pu, pi, pq = run(False, tok, cot, full, (vec, inner))
+        output, tokens_grad, pu, pi, pk, pq = run(False, tok, cot, full, (vec, inner))
 
         def whole(part, rows):
             return part.transpose(2, 1, 0, 3, 4).reshape(SHARDS * 2 * rows, D)
 
         parts = [
             whole(pq[:, :, :, 0:32], 32),
-            whole(pq[:, :, :, 32:64], 32),
-            whole(pq[:, :, :, 64:96], 32),
+            whole(pk[:, :, :, 0:32], 32),
+            whole(pk[:, :, :, 32:64], 32),
             whole(pi[:, :, :, 128:160], 32),
             pi[:, :, :, 0:128]
             .reshape(2, 2, 4, 4, 32, D)
@@ -893,8 +954,8 @@
             .reshape(D, FF),
             whole(pu, 128),
         ]
-        vecs = pq[0, :, :, 96:104, 0:64].transpose(2, 1, 0, 3).reshape(8, D)
-        inner = pq[1, :, :, 96, 0:256].transpose(1, 0, 2).reshape(FF)
+        vecs = pq[0, :, :, 32:40, 0:64].transpose(2, 1, 0, 3).reshape(8, D)
+        inner = pq[1, :, :, 32, 0:256].transpose(1, 0, 2).reshape(FF)
         parts += [vecs[j] for j in range(8)] + [inner]
         count = lax.axis_size("fsdp")
         packed = jnp.concatenate(

time: 151 us -> 139 us (0.921)
  Pallas kernels: 147 us -> 136 us
    pallas_call x1, Pallas kernels: 143 us -> 132 us  [run(): pl.pallas_call(functools.partial(layer, ring, blk), out_shape=outs, in_sp...]
where the time goes in v3:
time: 139 us; the launch traced here: 138 us
  Pallas kernels  136 us (98%)
    pallas_call x1, Pallas kernels, run(): pl.pallas_call(functools.partial(layer, ring, blk), out_shape=outs, in_sp...  132 us
    pallas_call x1, Pallas kernels, finish_all(): pl.pallas_call(finish_kernel, out_shape=outs, in_specs=[vmem_spec] * 6, o...  3.92 us

profile of v3, /device:TPU:0, one launch (start us, length us, event | category | flops | bytes accessed | tf_op | source)
XLA Modules:
  0.0 138.5 jit_solution(4659219644460999943)
XLA Ops:
  0.7 0.0 copy-start.8
  0.7 0.0 copy-start.7
  0.7 0.0 copy-start.3
  0.7 0.0 copy-start.4
  0.7 0.0 copy-start.5
  0.7 0.0 copy-start.6
  0.7 0.6 copy-done.8
  1.3 0.0 copy-start
  1.3 0.0 copy-start.1
  1.3 0.0 copy-start.2
  1.3 0.0 copy-done.7
  1.3 0.0 copy-done.3
  1.3 0.0 copy-done.4
  1.4 0.0 copy-done.5
  1.4 0.0 copy-done.6
  1.4 0.6 copy-done
  2.0 0.0 copy-done.1
  2.0 0.0 copy-done.2
  2.0 0.6 pad_maximum_fusion.refs_5_
  2.7 131.7 %layer.1 = (bf16[2,384,512]{2,1,0:T(8,128)(2,1)}, bf16[2,384,512]{2,1,0:T(8,128)(2,1)}, bf16[2,128,512]{2,1,0:T(8,128)(2,1)}, bf16[2,160,512]{2,1,0:T(8,128)(2,1...) custom-call(bf16[2,384,512]{2,1,0:T(8,128)(2,1)} %bitcast.35, bf16[2,384,512]{2,1,0:T(8,128)(2,1)} %bitcast.36, ...), custom_call_target="tpu_custom_call" | custom-call | tf_op jit(solution)/shard_map/layer/pallas_call | solution.py:855
  134.3 3.9 %finish.1 = (bf16[2,384,512]{2,1,0:T(8,128)(2,1)}, bf16[2,384,512]{2,1,0:T(8,128)(2,1)}, f32[64,512]{1,0:T(8,128)}, f32[64,512]{1,0:T(8,128)}, f32[64,512]{1,0:T...) custom-call(bf16[2,384,512]{2,1,0:T(8,128)(2,1)} %get-tuple-element., ...), custom_call_target="tpu_custom_call" | custom-call | tf_op jit(solution)/shard_map/finish/pallas_call | solution.py:902
  (3 shorter events, 0.0 us)
Async XLA Ops:
  0.7 0.7 copy-start.8
  0.7 0.7 copy-start.7
  0.7 0.7 copy-start.3
  0.7 0.7 copy-start.4
  0.7 0.7 copy-start.5
  0.7 0.7 copy-start.6
  1.3 0.7 copy-start
  1.3 0.7 copy-start.1
  1.3 0.7 copy-start.2

commit v4 on v3

--- a/solution.py
+++ b/solution.py
@@ -63,11 +63,11 @@
     W = next(it)
     vec, vec_inner = take(2)
     Q, QTa, dO, dOTa = take(4)
-    VTa, KT = take(2)
+    VTa = next(it)
     top, acc, OT = take(3)
     Hlow, n1, rstd1 = take(3)
     Z, dU, dF, dR, dA = take(5)
-    dwk, dwv = take(2)
+    dwkv = next(it)
     dka, dva = n1.at[0], n1.at[1]
     sums, sums_inner = take(2)
     cot_v = next(it)
@@ -242,6 +242,9 @@
     def weight(at, rows=32):
         return W[:, :, :, at : at + rows, :].reshape(SHARDS * 2 * rows, D)
 
+    def key_value_weight():
+        return jnp.concatenate([weight(AT_KEY), weight(AT_VALUE)], axis=1)
+
     b_query, b_value, b_out, gain1, shift1, b_outer, gain2, shift2 = (
         vec[pl.ds(j, 1), :] for j in range(8)
     )
@@ -313,8 +316,9 @@
 
     def keys_values(kb):
         x = X[kb]
-        K[kb] = dot(x, weight(AT_KEY)).astype(BF)
-        v = dot(x, weight(AT_VALUE)) + b_value
+        kv = dot(x, key_value_weight())
+        K[kb] = kv[:, :D].astype(BF)
+        v = kv[:, D:] + b_value
         V[kb] = v.astype(BF)
         vt = v.T.astype(BF)
         for h in range(HEADS):
@@ -480,11 +484,19 @@
                 parts + [jnp.zeros((13, blk), BF)], axis=0
             )
 
-    running = [dense(0), dense(1)]
-    if not ring:
-        list(running.pop(0))
-    while running:
-        running = [work for work in running if next(work, 0) is None]
+    sections = [dense(0), dense(1)]
+
+    def advance(stages):
+        for _ in range(stages):
+            for work in sections:
+                next(work, 0)
+
+    advance(5)
+
+    @pl.when(t >= 0)
+    def _():
+        advance(6)
+
     out_copy = pltpu.make_async_copy(cot_v, out_ref, out_sem.at[0])
     out_copy.start()
 
@@ -597,8 +609,7 @@
         reduce_y(0)
 
     acc[...] = jnp.zeros(acc.shape, F32)
-    dwk[...] = jnp.zeros(dwk.shape, F32)
-    dwv[...] = jnp.zeros(dwv.shape, F32)
+    dwkv[...] = jnp.zeros(dwkv.shape, F32)
 
     def attend_back(sec, kb, diagonal):
         def scores(h):
@@ -617,7 +628,7 @@
             return probs.astype(BF), (probs * dp).astype(BF)
 
         def to_queries(h, d_s):
-            acc[sec, h, 0:64, :] += dot(KT[h * 64 : h * 64 + 64, :], d_s)
+            acc[sec, h, 0:64, :] += dot(VTa[h, 0:64, :], d_s)
 
         def to_keys(p, first, second):
             cols = slice(p * 128, p * 128 + 128)
@@ -650,12 +661,31 @@
         far_out[sec] = (far_out[sec].astype(F32) + rel_in[sec].astype(F32)).astype(BF)
         to(far_out.at[sec], far_in.at[sec], ds.at[4 + sec], dr.at[4 + sec], ctx=far).start()
 
+    def send_back(i, owner_sec, dx):
+        low = dx.astype(BF)
+
+        @pl.when(i < 2)
+        def _():
+            rel_out[owner_sec] = low
+            to(rel_out.at[owner_sec], rel_in.at[owner_sec], ds.at[2 + owner_sec], dr.at[2 + owner_sec], ctx=sib).start()
+
+        @pl.when((i == 2) | (i == 3))
+        def _():
+            far_out[owner_sec] = low
+
+        @pl.when(i >= 4)
+        def _():
+            sib_out[owner_sec] = low
+            to(sib_out.at[owner_sec], sib_in.at[owner_sec], ds.at[owner_sec], dr.at[owner_sec], ctx=sib).start()
+
     def backward(i, _):
         owner_sec, owner, kb, sent, used = step_of(i)
 
         @pl.when(used)
         def _():
-            KT[...] = K[kb].astype(F32).T.astype(BF)
+            kt = K[kb].astype(F32).T.astype(BF)
+            for h in range(HEADS):
+                VTa[h, 0:64, :] = kt[h * 64 : h * 64 + 64]
             dka[...] = jnp.zeros(dka.shape, F32)
             dva[...] = jnp.zeros(dva.shape, F32)
 
@@ -676,31 +706,18 @@
 
         @pl.when(used)
         def _():
-            dk = (dka[...] * LN2).astype(BF)
-            dv = dva[...].astype(BF)
-            x = X[kb]
-            dwk[...] += dot(x, dk, 0, 0)
-            dwv[...] += dot(x, dv, 0, 0)
-            sums[1:2, :] += dot(ones, dv)[0:1]
-            dx = dot(dk, weight(AT_KEY), 1, 1) + dot(dv, weight(AT_VALUE), 1, 1)
-
-            @pl.when(i < 2)
+            both_low = jnp.concatenate([dka[...] * LN2, dva[...]], axis=1).astype(BF)
+            dwkv[...] += dot(X[kb], both_low, 0, 0)
+            sums[1:2, :] += column_sum(dva[...])
+
+            @pl.when(i < 6)
             def _():
-                rel_out[owner_sec] = dx.astype(BF)
-                to(rel_out.at[owner_sec], rel_in.at[owner_sec], ds.at[2 + owner_sec], dr.at[2 + owner_sec], ctx=sib).start()
-
-            @pl.when((i == 2) | (i == 3))
-            def _():
-                far_out[owner_sec] = dx.astype(BF)
-
-            @pl.when((i == 4) | (i == 5))
-            def _():
-                sib_out[owner_sec] = dx.astype(BF)
-                to(sib_out.at[owner_sec], sib_in.at[owner_sec], ds.at[owner_sec], dr.at[owner_sec], ctx=sib).start()
+                send_back(i, owner_sec, dot(both_low, key_value_weight(), 1, 1))
 
             @pl.when(i >= 6)
             def _():
-                dR[owner_sec] += dx
+                K[kb] = both_low[:, :D]
+                V[kb] = both_low[:, D:]
 
         @pl.when(i == 3)
         def _():
@@ -711,15 +728,16 @@
             pl.when(i == 0)(functools.partial(reduce_y, 1))
             pl.when(i == 2)(functools.partial(reduce_z, 0, 0, 2))
             pl.when(i == 3)(functools.partial(reduce_z, 0, 2, 4))
-            pl.when(i == 5)(functools.partial(reduce_z, 1, 0, 2))
-            pl.when(i == 6)(functools.partial(reduce_z, 1, 2, 4))
+            pl.when(i == 3)(functools.partial(reduce_z, 1, 0, 1))
+            pl.when(i == 4)(functools.partial(reduce_z, 1, 1, 2))
+            pl.when(i == 5)(functools.partial(reduce_z, 1, 2, 4))
             pl.when(i == 6)(functools.partial(reduce_x, 0))
         return 0
 
     lax.fori_loop(0, 8, backward, 0)
 
-    by_owner(PK, dwk[...].astype(BF), 0)
-    by_owner(PK, dwv[...].astype(BF), 32)
+    by_owner(PK, dwkv[:, :D].astype(BF), 0)
+    by_owner(PK, dwkv[:, D:].astype(BF), 32)
     if ring:
         reduce_core(2)
 
@@ -749,11 +767,19 @@
         reduce_core(3)
         reduce_y(2)
         reduce_y(3)
-
-    for sec in range(2):
-        dx = dR[sec] + dot(Q[sec], weight(AT_QUERY), 1, 1)
-        tg_v[sec] = dx.astype(BF)
-        dR[sec] = dx
+        reduce_last(0)
+        reduce_x(1)
+
+    def own_tokens(sec, _):
+        kb = jnp.where(sec == 0, c, 7 - c)
+        dR[sec] += (
+            dot(Q[sec], weight(AT_QUERY), 1, 1)
+            + dot(K[kb], weight(AT_KEY), 1, 1)
+            + dot(V[kb], weight(AT_VALUE), 1, 1)
+        )
+        return 0
+
+    lax.fori_loop(0, 2, own_tokens, 0)
 
     def add_incoming(ref, sem, sec):
         arrived(ref.at[sec], sem)
@@ -771,8 +797,6 @@
     if ring:
         reduce_z(2)
         reduce_z(3)
-        reduce_x(1)
-        reduce_last(0)
         for u in range(6):
             gather_left(u)
         reduce_last(1)
@@ -834,11 +858,11 @@
     scratch += [vm(4, 2, 2, PACKED, D)]
     scratch += [vf(8, D), vf(1, FF)]
     scratch += [vm(2, blk, D), vm(2, HEADS, 128, blk)] * 2
-    scratch += [vm(HEADS, 80, blk), vm(D, blk)]
+    scratch += [vm(HEADS, 80, blk)]
     scratch += [vf(2, HEADS, 8, blk), vf(2, HEADS, 80, blk), vm(2, D, blk)]
     scratch += [vm(2, blk, D), vf(2, blk, D), vf(2, blk, 1)]
     scratch += [vm(2, blk, FF)] * 2 + [vm(2, blk, D), vf(2, blk, D), vm(2, blk, D)]
-    scratch += [vf(D, D)] * 2
+    scratch += [vf(D, 2 * D)]
     scratch += [vf(8, D), vf(8, FF)]
     scratch += [vm(2, blk, D)]
     scratch += [vm(2, 2, 4, rows, D) for rows in GROUP_ROWS]

time: 139 us -> 133 us (0.957)
  Pallas kernels: 136 us -> 130 us
    pallas_call x1, Pallas kernels: 132 us -> 126 us  [run(): pl.pallas_call(functools.partial(layer, ring, blk), out_shape=outs, in_sp...]
where the time goes in v4:
time: 133 us
  Pallas kernels  130 us (98%)
    pallas_call x1, Pallas kernels, run(): pl.pallas_call(functools.partial(layer, ring, blk), out_shape=outs, in_sp...  126 us
    pallas_call x1, Pallas kernels, finish_all(): pl.pallas_call(finish_kernel, out_shape=outs, in_specs=[vmem_spec] * 6, o...  3.92 us

profile of v4, /device:TPU:0, one launch (start us, length us, event | category | flops | bytes accessed | tf_op | source)
XLA Modules:
  0.0 132.5 jit_solution(2989934201239229288)
XLA Ops:
  0.7 0.0 copy-start.8
  0.7 0.0 copy-start.7
  0.7 0.0 copy-start.3
  0.7 0.0 copy-start.4
  0.7 0.0 copy-start.5
  0.7 0.0 copy-start.6
  0.7 0.6 copy-done.8
  1.3 0.0 copy-start
  1.3 0.0 copy-start.1
  1.3 0.0 copy-start.2
  1.3 0.0 copy-done.7
  1.3 0.0 copy-done.3
  1.3 0.0 copy-done.4
  1.4 0.0 copy-done.5
  1.4 0.0 copy-done.6
  1.4 0.6 copy-done
  2.0 0.0 copy-done.1
  2.0 0.0 copy-done.2
  2.0 0.6 pad_maximum_fusion.refs_5_
  2.7 125.7 %layer.1 = (bf16[2,384,512]{2,1,0:T(8,128)(2,1)}, bf16[2,384,512]{2,1,0:T(8,128)(2,1)}, bf16[2,128,512]{2,1,0:T(8,128)(2,1)}, bf16[2,160,512]{2,1,0:T(8,128)(2,1...) custom-call(bf16[2,384,512]{2,1,0:T(8,128)(2,1)} %bitcast.35, bf16[2,384,512]{2,1,0:T(8,128)(2,1)} %bitcast.36, ...), custom_call_target="tpu_custom_call" | custom-call | tf_op jit(solution)/shard_map/layer/pallas_call | solution.py:879
  128.4 3.9 %finish.1 = (bf16[2,384,512]{2,1,0:T(8,128)(2,1)}, bf16[2,384,512]{2,1,0:T(8,128)(2,1)}, f32[64,512]{1,0:T(8,128)}, f32[64,512]{1,0:T(8,128)}, f32[64,512]{1,0:T...) custom-call(bf16[2,384,512]{2,1,0:T(8,128)(2,1)} %get-tuple-element., ...), custom_call_target="tpu_custom_call" | custom-call | tf_op jit(solution)/shard_map/finish/pallas_call | solution.py:926
  (3 shorter events, 0.0 us)
Async XLA Ops:
  0.7 0.7 copy-start.8
  0.7 0.7 copy-start.7
  0.7 0.7 copy-start.3
  0.7 0.7 copy-start.4
  0.7 0.7 copy-start.5
  0.7 0.7 copy-start.6
  1.3 0.7 copy-start
  1.3 0.7 copy-start.1
  1.3 0.7 copy-start.2

commit v5 on v4

--- a/solution.py
+++ b/solution.py
@@ -22,19 +22,7 @@
 LN2 = math.log(2.0)
 AT_QUERY, AT_KEY, AT_VALUE, AT_SMALL, AT_OUT, AT_INNER, AT_OUTER, PACKED = 0, 32, 64, 96, 112, 144, 272, 400
 UNITS = ((0, 32), (32, 64), (64, 112), (112, 208), (208, 304), (304, 400))
-GATHER_AT = (
-    (0, 3, 1),
-    (1, 4, 1),
-    (2, 5, 1),
-    (3, 3, 2),
-    (4, 4, 2),
-    (6, 5, 2),
-    (7, 3, 3),
-    (9, 4, 3),
-    (11, 5, 3),
-    (12, 3, 0),
-    (15, 4, 0),
-)
+GATHER_AT = ((0, 3, 1), (1, 4, 1), (2, 5, 1), (4, 3, 2), (5, 4, 2), (7, 5, 2), (8, 3, 3), (10, 4, 3), (12, 5, 3), (13, 3, 0), (15, 4, 0))
 GROUP_ROWS = (128, 160, 64, 48)
 
 
@@ -748,6 +736,8 @@
         return 0
 
     lax.fori_loop(0, 2, d_query, 0)
+    if ring:
+        reduce_y(2)
     xx = jnp.concatenate([X[c], X[7 - c]], axis=0)
     by_owner(PQ, dot(xx, both(Q), 0, 0).astype(BF), 0)
     for s in range(SHARDS):
@@ -765,7 +755,6 @@
         ).astype(BF)
     if ring:
         reduce_core(3)
-        reduce_y(2)
         reduce_y(3)
         reduce_last(0)
         reduce_x(1)
@@ -794,11 +783,25 @@
     tg_copy = pltpu.make_async_copy(tg_v, tg_ref, out_sem.at[1])
     tg_copy.start()
 
+    block = X.at[0]
+    for k in range(3):
+        left(block, xs.at[k])
+    pl.when(chip == 1)(lambda: left(block, xs.at[3]))
+    left(block, xs.at[4])
+    pl.when(chip == 0)(lambda: left(block, xs.at[5]))
+    left(block, ds.at[0])
+    pl.when(core == 0)(lambda: left(block, ds.at[1]))
+    left(block, ds.at[2])
+    pl.when(chip == 0)(lambda: left(block, ds.at[3]))
+    left(block, ds.at[4])
+    pl.when(chip == 0)(lambda: left(block, ds.at[5]))
+    if ring:
+        for u in range(6):
+            gather_left(u)
+
     if ring:
         reduce_z(2)
         reduce_z(3)
-        for u in range(6):
-            gather_left(u)
         reduce_last(1)
         reduce_x(2)
         reduce_x(3)
@@ -822,18 +825,6 @@
         for copy in copies:
             copy.wait()
 
-    block = X.at[0]
-    for k in range(3):
-        left(block, xs.at[k])
-    pl.when(chip == 1)(lambda: left(block, xs.at[3]))
-    left(block, xs.at[4])
-    pl.when(chip == 0)(lambda: left(block, xs.at[5]))
-    left(block, ds.at[0])
-    pl.when(core == 0)(lambda: left(block, ds.at[1]))
-    left(block, ds.at[2])
-    pl.when(chip == 0)(lambda: left(block, ds.at[3]))
-    left(block, ds.at[4])
-    pl.when(chip == 0)(lambda: left(block, ds.at[5]))
     out_copy.wait()
     tg_copy.wait()
 

time: 133 us -> 133 us (level)
  no operation moved by 1% of the time
where the time goes in v5:
time: 133 us; the launch traced here: 132 us
  Pallas kernels  129 us (97%)
    pallas_call x1, Pallas kernels, run(): pl.pallas_call(functools.partial(layer, ring, blk), out_shape=outs, in_sp...  125 us
    pallas_call x1, Pallas kernels, finish_all(): pl.pallas_call(finish_kernel, out_shape=outs, in_specs=[vmem_spec] * 6, o...  3.92 us

profile of v5, /device:TPU:0, one launch (start us, length us, event | category | flops | bytes accessed | tf_op | source)
XLA Modules:
  0.0 131.7 jit_solution(722730661090497851)
XLA Ops:
  0.7 0.0 copy-start.8
  0.7 0.0 copy-start.7
  0.7 0.0 copy-start.3
  0.7 0.0 copy-start.4
  0.7 0.0 copy-start.5
  0.7 0.0 copy-start.6
  0.7 0.6 copy-done.8
  1.3 0.0 copy-start
  1.3 0.0 copy-start.1
  1.3 0.0 copy-start.2
  1.3 0.0 copy-done.7
  1.3 0.0 copy-done.3
  1.3 0.0 copy-done.4
  1.4 0.0 copy-done.5
  1.4 0.0 copy-done.6
  1.4 0.6 copy-done
  2.0 0.0 copy-done.1
  2.0 0.0 copy-done.2
  2.0 0.6 pad_maximum_fusion.refs_5_
  2.7 124.9 %layer.1 = (bf16[2,384,512]{2,1,0:T(8,128)(2,1)}, bf16[2,384,512]{2,1,0:T(8,128)(2,1)}, bf16[2,128,512]{2,1,0:T(8,128)(2,1)}, bf16[2,160,512]{2,1,0:T(8,128)(2,1...) custom-call(bf16[2,384,512]{2,1,0:T(8,128)(2,1)} %bitcast.35, bf16[2,384,512]{2,1,0:T(8,128)(2,1)} %bitcast.36, ...), custom_call_target="tpu_custom_call" | custom-call | tf_op jit(solution)/shard_map/layer/pallas_call | solution.py:870
  127.6 3.9 %finish.1 = (bf16[2,384,512]{2,1,0:T(8,128)(2,1)}, bf16[2,384,512]{2,1,0:T(8,128)(2,1)}, f32[64,512]{1,0:T(8,128)}, f32[64,512]{1,0:T(8,128)}, f32[64,512]{1,0:T...) custom-call(bf16[2,384,512]{2,1,0:T(8,128)(2,1)} %get-tuple-element., ...), custom_call_target="tpu_custom_call" | custom-call | tf_op jit(solution)/shard_map/finish/pallas_call | solution.py:917
  (3 shorter events, 0.0 us)
Async XLA Ops:
  0.7 0.7 copy-start.8
  0.7 0.7 copy-start.7
  0.7 0.7 copy-start.3
  0.7 0.7 copy-start.4
  0.7 0.7 copy-start.5
  0.7 0.7 copy-start.6
  1.3 0.7 copy-start
  1.3 0.7 copy-start.1
  1.3 0.7 copy-start.2
